TPU v7x, 128 devices: a whole 4x4x4 slice. The times are simulated.
128 devices in a mesh: seq: 128 (over z, y, x, core).
Axes of the slice: x: 4, y: 4, z: 4, core: 2. Of those that a mesh axis runs over, the one named last changes fastest.
Arguments:
- query_points: bfloat16 [65536, 512], P('seq'), may hold values from -6 to 6
- key_points: bfloat16 [65536, 512], P('seq'), may hold values from -6 to 6
- value_points: bfloat16 [65536, 512], P('seq'), may hold values from -6 to 6
- cotangent: bfloat16 [65536, 512], P('seq'), may hold values from -6 to 6
- hilbert_order: int32 [65536], P('seq'), may hold values from 0 to 65535, as said below
Outputs:
- attended: bfloat16 [65536, 512], P('seq')
- query_grad: bfloat16 [65536, 512], P('seq')
- key_grad: bfloat16 [65536, 512], P('seq')
- value_grad: bfloat16 [65536, 512], P('seq')
Inputs may be any that keep to these rules, and one draw needn't show every extreme that they name: `hilbert_order`: within each aligned block of 512 positions, the entries are a permutation of that block's own indices.
All inputs are finite; a program needn't handle non-finite values.
Results may differ from a plain program's by a relative error of at most 0.012.
The roundings to bfloat16 on the way count: a program that leaves them out, or rounds other values in their place, can miss the bound.
Values may be sent and summed in bfloat16 or wider, within the bound.
A program may use at most 128 MiB of HBM per device.

v0:
```python
import jax
import jax.numpy as jnp
from jax import lax
from jax.sharding import PartitionSpec as P

HEADS = 8
HEAD_DIM = 64
FEAT = 512
BLOCK_ROWS = 128
POOL = 4


NEG = -1e30


def extended(block, sides, width):
    for axis, dim in sides:
        count = lax.axis_size(axis)
        forward = [(i, i + 1) for i in range(count - 1)]
        backward = [(target, source) for source, target in forward]
        low = lax.ppermute(
            lax.slice_in_dim(block, block.shape[dim] - width, None, axis=dim), axis, forward
        )
        high = lax.ppermute(lax.slice_in_dim(block, 0, width, axis=dim), axis, backward)
        block = jnp.concatenate([low, block, high], axis=dim)
    return block


def passed_along(value, axis, steps):
    count = lax.axis_size(axis)
    initial, last = (max(0, -steps), min(count, count - steps))
    return lax.ppermute(value, axis, [(source, source + steps) for source in range(initial, last)])


def split_heads(value_rows):
    return value_rows.reshape(value_rows.shape[:-1] + (HEADS, HEAD_DIM))


def pooled(rows, factor, average):
    if factor == 1:
        return rows
    grouped = jnp.sum(
        rows.reshape(rows.shape[0] // factor, factor, rows.shape[1]), axis=1, dtype=jnp.float32
    )
    if average:
        grouped = grouped / factor
    return grouped.astype(jnp.bfloat16)


def permitted(qpos, kpos, level, count):
    upper = qpos[..., :, None]
    lower = kpos[..., None, :]
    inside = (lower >= 0) & (lower < count) & (upper >= 0) & (upper < count)
    near = jnp.abs(upper // BLOCK_ROWS - lower // BLOCK_ROWS) <= 1
    if level > 0:
        width = BLOCK_ROWS // POOL
        near = near & (jnp.abs(upper // width - lower // width) > 1)
    return inside & near


def scores_of(query, keys, allow):
    raw = jnp.einsum(
        "bqhd,bkhd->bhqk", split_heads(query), split_heads(keys), preferred_element_type=jnp.float32
    )
    return jnp.where(allow[:, None], raw * HEAD_DIM ** (-0.5), NEG)


def level_forward(query, keys, value_rows, allow, factor):
    scores = scores_of(query, keys, allow)
    top = jnp.max(scores, axis=3)
    weights = jnp.exp(scores - top[..., None])
    numer = jnp.einsum(
        "bhqk,bkhd->bqhd",
        weights.astype(jnp.bfloat16),
        split_heads(value_rows),
        preferred_element_type=jnp.float32,
    )
    total = factor * jnp.sum(weights, axis=3)
    count = query.shape[0] * query.shape[1]
    return (
        numer.reshape(count, FEAT),
        jnp.swapaxes(total, 1, 2).reshape(count, HEADS),
        jnp.swapaxes(top, 1, 2).reshape(count, HEADS),
    )


def pair_terms(query, keys, value_rows, allow, factor, top, gsum, esum):
    scores = scores_of(query, keys, allow)
    weights = jnp.exp(scores - jnp.swapaxes(top, 1, 2)[..., None])
    mixing = jnp.einsum(
        "bqhd,bkhd->bhqk",
        split_heads(gsum),
        split_heads(value_rows),
        preferred_element_type=jnp.float32,
    )
    dscore = (weights * (mixing - factor * jnp.swapaxes(esum, 1, 2)[..., None])).astype(
        jnp.bfloat16
    )
    return (weights, dscore)


def level_backward(query, keys, value_rows, allow, factor, top, gsum, esum):
    weights, dscore = pair_terms(query, keys, value_rows, allow, factor, top, gsum, esum)
    grads_split = split_heads(gsum)
    value_terms = jnp.einsum(
        "bhqk,bqhd->bkhd",
        weights.astype(jnp.bfloat16),
        grads_split,
        preferred_element_type=jnp.float32,
    )
    scale = HEAD_DIM ** (-0.5)
    query_terms = scale * jnp.einsum(
        "bhqk,bkhd->bqhd", dscore, split_heads(keys), preferred_element_type=jnp.float32
    )
    key_terms = scale * jnp.einsum(
        "bhqk,bqhd->bkhd", dscore, split_heads(query), preferred_element_type=jnp.float32
    )
    blocks, width, span = (query.shape[0], query.shape[1], keys.shape[1])
    return (
        query_terms.reshape(blocks, width, FEAT),
        key_terms.reshape(blocks, span, FEAT),
        value_terms.reshape(blocks, span, FEAT),
    )


def rim_rows(pair):
    return extended(pair, (("seq", 1),), BLOCK_ROWS)


def rim_back(value_rows, offset):
    return passed_along(value_rows.astype(jnp.bfloat16), "seq", offset).astype(value_rows.dtype)


def far_shift(value_rows, offset):
    return passed_along(value_rows, "seq", offset)


def far_back(value_rows, offset):
    return passed_along(value_rows.astype(jnp.bfloat16), "seq", offset).astype(value_rows.dtype)


def block_windows(padded, count):
    blocks = count // BLOCK_ROWS
    lead = padded.shape[0]
    parts = [
        padded[:, part * BLOCK_ROWS : part * BLOCK_ROWS + count].reshape(
            lead, blocks, BLOCK_ROWS, padded.shape[2]
        )
        for part in range(3)
    ]
    return jnp.concatenate(parts, axis=2)


def fold_windows(grads, count):
    feat = grads.shape[-1]
    padded = jnp.zeros((2, count + 2 * BLOCK_ROWS, feat), jnp.float32)
    for part in range(3):
        piece = grads[:, :, part * BLOCK_ROWS : (part + 1) * BLOCK_ROWS].reshape(2, count, feat)
        padded = padded + jnp.pad(
            piece, ((0, 0), (part * BLOCK_ROWS, (2 - part) * BLOCK_ROWS), (0, 0))
        )
    inner = padded[:, BLOCK_ROWS : BLOCK_ROWS + count]
    from_right = rim_back(padded[:, :BLOCK_ROWS], -1)
    from_left = rim_back(padded[:, BLOCK_ROWS + count :], 1)
    inner = inner + jnp.pad(from_left, ((0, 0), (0, count - BLOCK_ROWS), (0, 0)))
    return inner + jnp.pad(from_right, ((0, 0), (count - BLOCK_ROWS, 0), (0, 0)))


def far_keys(pair, index, count):
    steps = (2 * BLOCK_ROWS // count - 1).bit_length()
    behind = pair
    ahead = pair
    for bit in range(steps):
        behind = jnp.concatenate([far_shift(behind, 2**bit), behind], axis=1)
        ahead = jnp.concatenate([ahead, far_shift(ahead, -(2**bit))], axis=1)
    window = jnp.concatenate([behind, ahead[:, count:]], axis=1)
    start_index = (index - (2**steps - 1)) * count
    return (window, start_index)


def far_fold(grads, count):
    steps = (2 * BLOCK_ROWS // count - 1).bit_length()
    reach = 2**steps - 1
    behind = grads[:, : (reach + 1) * count]
    ahead = jnp.concatenate(
        [jnp.zeros_like(grads[:, :count]), grads[:, (reach + 1) * count :]], axis=1
    )
    for bit in reversed(range(steps)):
        half = 2**bit * count
        behind = behind[:, half:] + far_back(behind[:, :half], -(2**bit))
        ahead = ahead[:, :half] + far_back(ahead[:, half:], 2**bit)
    return behind + ahead


def on_device(query_points, key_points, value_points, cotangent, hilbert_order):
    rows = query_points.shape[0]
    devices = lax.axis_size("seq")
    index = lax.axis_index("seq")
    local = hilbert_order - index * rows
    ordered = jnp.take(
        jnp.stack([query_points, key_points, value_points, cotangent]), local, axis=1
    )
    level_list = []
    for level in range(3):
        factor = POOL**level
        count = rows // factor
        query = pooled(ordered[0], factor, True)
        pair = jnp.stack([pooled(ordered[1], factor, True), pooled(ordered[2], factor, False)])
        query_window = None
        if level < 2:
            blocks = count // BLOCK_ROWS
            windows = block_windows(rim_rows(pair), count)
            queries = query.reshape(blocks, BLOCK_ROWS, FEAT)
            qpos = index * count + jnp.arange(count, dtype=jnp.int32).reshape(blocks, BLOCK_ROWS)
            kpos = qpos[:, :1] - BLOCK_ROWS + jnp.arange(3 * BLOCK_ROWS, dtype=jnp.int32)[None, :]
        else:
            window, start_index = far_keys(pair, index, count)
            windows = window[:, None]
            queries = query[None]
            qpos = (index * count + jnp.arange(count, dtype=jnp.int32))[None]
            kpos = (start_index + jnp.arange(window.shape[1], dtype=jnp.int32))[None]
        allow = permitted(qpos, kpos, level, count * devices)
        numer, total, top = level_forward(queries, windows[0], windows[1], allow, factor)
        level_list.append(
            (factor, queries, windows, allow, numer, total, top, query_window, qpos, kpos)
        )
    tops = [jnp.repeat(item[6], item[0], axis=0) for item in level_list]
    best = jnp.maximum(jnp.maximum(tops[0], tops[1]), tops[2])
    scales = [jnp.exp(top - best) for top in tops]
    denom = scales[0] * jnp.repeat(level_list[0][5], level_list[0][0], axis=0)
    denom = denom + scales[1] * jnp.repeat(level_list[1][5], level_list[1][0], axis=0)
    denom = denom + scales[2] * jnp.repeat(level_list[2][5], level_list[2][0], axis=0)
    mixed = scales[0][..., None] * split_heads(
        jnp.repeat(level_list[0][4], level_list[0][0], axis=0)
    )
    mixed = mixed + scales[1][..., None] * split_heads(
        jnp.repeat(level_list[1][4], level_list[1][0], axis=0)
    )
    mixed = mixed + scales[2][..., None] * split_heads(
        jnp.repeat(level_list[2][4], level_list[2][0], axis=0)
    )
    mixed = mixed / denom[..., None]
    upstream = split_heads(ordered[3].astype(jnp.float32))
    delta = jnp.sum(upstream * mixed, axis=2)
    query_sum = jnp.zeros((rows, FEAT), jnp.float32)
    key_sum = jnp.zeros((rows, FEAT), jnp.float32)
    value_sum = jnp.zeros((rows, FEAT), jnp.float32)
    for level in range(3):
        factor, queries, windows, allow, numer, total, top, query_window, qpos, kpos = level_list[
            level
        ]
        count = rows // factor
        blocks, width = (queries.shape[0], queries.shape[1])
        share = scales[level] / denom
        gsum = jnp.sum((share[..., None] * upstream).reshape(count, factor, FEAT), axis=1).astype(
            jnp.bfloat16
        )
        esum = jnp.sum((share * delta).reshape(count, factor, HEADS), axis=1)
        top_blocks = top.reshape(blocks, width, HEADS)
        gsum_blocks = gsum.reshape(blocks, width, FEAT)
        esum_blocks = esum.reshape(blocks, width, HEADS)
        if level < 2:
            query_terms, key_terms, value_terms = level_backward(
                queries, windows[0], windows[1], allow, factor, top_blocks, gsum_blocks, esum_blocks
            )
            returned = fold_windows(jnp.stack([key_terms, value_terms]), count)
        else:
            query_terms, key_terms, value_terms = level_backward(
                queries, windows[0], windows[1], allow, factor, top_blocks, gsum_blocks, esum_blocks
            )
            returned = far_fold(jnp.stack([key_terms, value_terms])[:, 0], count)
        query_sum = (
            query_sum + jnp.repeat(query_terms.reshape(count, FEAT), factor, axis=0) / factor
        )
        key_sum = key_sum + jnp.repeat(returned[0], factor, axis=0) / factor
        value_sum = value_sum + jnp.repeat(returned[1], factor, axis=0)
    results = jnp.stack([mixed.reshape(rows, FEAT), query_sum, key_sum, value_sum]).astype(
        jnp.bfloat16
    )
    placed = jnp.zeros_like(results).at[:, local].set(results)
    return (placed[0], placed[1], placed[2], placed[3])


def solution(mesh):
    placed = (P("seq", None), P("seq", None), P("seq", None), P("seq", None), P("seq"))
    return jax.shard_map(
        on_device,
        mesh=mesh,
        in_specs=placed,
        out_specs=(P("seq", None), P("seq", None), P("seq", None), P("seq", None)),
        check_vma=False,
    )
```

profile of v0, /device:TPU:63, one launch (start us, length us, event | category | flops | bytes accessed | tf_op | source)
XLA Modules:
  0.0 406.0 jit_solution(13303033549937077776)
XLA Ops:
  7.4 5.4 %pad_maximum_fusion.2 = bf16[4,512,512]{2,0,1:T(4,128)(2,1)S(1)} fusion(bf16[1,512,512]{2,0,1:T(2,128)(2,1)S(1)} %copy.414, bf16[1,512,512]{2,0,1:T(2,128)(2,1)S(1)} %copy.413, bf16[1,512,512]{2,0,1:T(2,128)(2,1)S(1)} %copy.412, bf16[1,512,512]{2,0,1:T(2,128)(2,1)S(1)} %copy.411), kind=kLoop, calls=%fused_computation.25 | loop fusion | flops 8388608 | bytes 4194304 | tf_op jit(solution)/shard_map/stack | solution.py:201
  12.8 3.8 gather_fusion
  16.6 3.0 select_bitcast_fusion
  19.6 11.1 %slice_convert_fusion = (f32[1,512,512]{2,0,1:T(1,128)}, f32[1,512,512]{2,0,1:T(1,128)}, bf16[1,512,512]{2,0,1:T(2,128)(2,1)S(1)}, f32[1,512,512]{2,0,1:T(1,128)...) fusion(bf16[4,512,512]{2,0,1:T(4,128)(2,1)S(1)} %select_bitcast_fusion), kind=kLoop, calls=%fused_computation.64 | loop fusion | flops 786432 | bytes 6815744 | tf_op jit(solution)/shard_map/convert_element_type | solution.py:243
  36.1 3.7 collective-permute-start.4
  43.0 7.8 %collective-permute-start = (bf16[2,128,512]{2,0,1:T(2,128)(2,1)}, bf16[2,128,512]{2,0,1:T(2,128)(2,1)}, u32[]{:S(2)}, u32[]{:S(2)}) collective-permute-start(bf16[2,128,512]{2,0,1:T(2,128)(2,1)} %get-tuple-element.37), channel_id=1, source_target_pairs={{0,1},{1,2},{2,3},{3,4},{4,5},{5,6},{6,7},{7,8},{8,9},{9,10},{10,1... | collective-permute-start | bytes 786440 | tf_op jit(solution)/shard_map/ppermute | solution.py:21
  53.0 11.0 %fusion.108 = (f32[512,512]{1,0:T(8,128)}, f32[512,512]{1,0:T(8,128)}, f32[512,512]{1,0:T(8,128)}) fusion(bf16[4,512,512]{2,0,1:T(4,128)(2,1)S(1)} %select_bitcast_fusion), kind=kLoop, calls=%fused_computation.264 | loop fusion | flops 786432 | bytes 4718592 | tf_op jit(solution)/shard_map/convert_element_type | solution.py:243
  69.4 7.8 %collective-permute-start.2 = (bf16[2,128,512]{2,1,0:T(8,128)(2,1)}, bf16[2,128,512]{2,1,0:T(8,128)(2,1)}, u32[]{:S(2)}, u32[]{:S(2)}) collective-permute-start(bf16[2,128,512]{2,1,0:T(8,128)(2,1)} %get-tuple-element.60), channel_id=1, source_target_pairs={{0,1},{1,2},{2,3},{3,4},{4,5},{5,6},{6,7},{7,8},{8,9},{9,10},{10,1... | collective-permute-start | bytes 786440 | tf_op jit(solution)/shard_map/ppermute | solution.py:21
  89.4 2.7 reshape.1564
  107.1 3.4 collective-permute-start.8
  113.1 4.8 %collective-permute-done.8 = bf16[2,64,512]{2,1,0:T(8,128)(2,1)S(1)} collective-permute-done((bf16[2,64,512]{2,1,0:T(8,128)(2,1)S(1)}, bf16[2,64,512]{2,1,0:T(8,128)(2,1)S(1)}, u32[]{:S(2)}, u32[]{:S(2)}) %collective-permute-start.8) | collective-permute-done | bytes 131104 | tf_op jit(solution)/shard_map/ppermute | solution.py:32
  121.5 4.9 %collective-permute-start.9 = (bf16[2,128,512]{2,1,0:T(8,128)(2,1)}, bf16[2,128,512]{2,1,0:T(8,128)(2,1)}, u32[]{:S(2)}, u32[]{:S(2)}) collective-permute-start(bf16[2,128,512]{2,1,0:T(8,128)(2,1)} %get-tuple-element.61), channel_id=1, source_target_pairs={{4,0},{5,1},{6,2},{7,3},{8,4},{9,5},{10,6},{11,7},{12,8},{13,9},{1... | collective-permute-start | bytes 786440 | tf_op jit(solution)/shard_map/ppermute | solution.py:32
  126.4 4.8 %pad_maximum_fusion.5 = (bf16[2,512,512]{2,0,1:T(2,128)(2,1)}, bf16[2,512,512]{2,0,1:T(2,128)(2,1)S(1)}) fusion(bf16[2,512,512]{2,0,1:T(2,128)(2,1)S(1)} %stack.62, bf16[2,128,512]{2,0,1:T(2,128)(2,1)} %collective-permute-done, bf16[2,128,512]{2,0,1:T(2,128)(2,1)} %collective-permute-done.1), kind=kLoop, calls=%fused_computation.67 | loop fusion | flops 1048576 | bytes 3670016 | tf_op jit(solution)/shard_map/concatenate | solution.py:25
  131.2 3.8 copy.416
  140.7 2.9 fusion.101
  143.7 2.7 fusion.1
  157.4 3.3 reshape_reshape.10
  162.4 2.9 copy.426
  173.8 3.2 copy.449
  206.9 2.8 reshape_reshape.11
  209.7 3.2 copy.450
  213.6 2.7 fusion.28
  220.9 6.3 %fusion.35 = f32[4,8,64,384]{3,2,1,0:T(8,128)} fusion(bf16[4,128,8,64]{1,0,3,2:T(4,128)(2,1)S(1)} %multiply_convert_fusion.2, f32[4,8,128,384]{3,2,1,0:T(8,128)} %copy-done, f32[4,8,128]{2,1,0:T(8,128)S(1)} %get-tuple-element.69, pred[4,128,384]{2,1,0:T(8,128)(4,1)S(1)} %copy-done.28), kind=kOutput, calls=%fused_computation.108 | convolution fusion | flops 207618048 | bytes 10174464 | tf_op jit(solution)/shard_map/bhqk,bqhd->bkhd/dot_general | solution.py:105
  227.2 2.7 multiply_convert_fusion
  270.5 6.7 %collective-permute-start.12 = (bf16[2,128,512]{1,2,0:T(8,128)(2,1)}, bf16[2,128,512]{1,2,0:T(8,128)(2,1)}, u32[]{:S(2)}, u32[]{:S(2)}) collective-permute-start(bf16[2,128,512]{1,2,0:T(8,128)(2,1)} %get-tuple-element.51), channel_id=1, source_target_pairs={{0,1},{1,2},{2,3},{3,4},{4,5},{5,6},{6,7},{7,8},{8,9},{9,10},{10,1... | collective-permute-start | bytes 786440 | tf_op jit(solution)/shard_map/ppermute | solution.py:32
  284.6 8.0 %collective-permute-start.17 = (bf16[2,128,512]{1,2,0:T(8,128)(2,1)}, bf16[2,128,512]{1,2,0:T(8,128)(2,1)}, u32[]{:S(2)}, u32[]{:S(2)}) collective-permute-start(bf16[2,128,512]{1,2,0:T(8,128)(2,1)} %get-tuple-element.46), channel_id=1, source_target_pairs={{0,4},{1,5},{2,6},{3,7},{4,8},{5,9},{6,10},{7,11},{8,12},{9,13},{1... | collective-permute-start | bytes 786440 | tf_op jit(solution)/shard_map/ppermute | solution.py:32
  307.1 7.6 %collective-permute-start.18 = (bf16[2,64,512]{1,2,0:T(8,128)(2,1)S(1)}, bf16[2,64,512]{1,2,0:T(8,128)(2,1)S(1)}, u32[]{:S(2)}, u32[]{:S(2)}) collective-permute-start(bf16[2,64,512]{1,2,0:T(8,128)(2,1)S(1)} %slice.371), channel_id=1, source_target_pairs={{0,2},{1,3},{2,4},{3,5},{4,6},{5,7},{6,8},{7,9},{8,10},{9,11},{10,... | collective-permute-start | bytes 393224 | tf_op jit(solution)/shard_map/ppermute | solution.py:32
  319.4 3.5 collective-permute-start.16
  324.0 6.4 %collective-permute-start.19 = (bf16[2,32,512]{1,2,0:T(8,128)(2,1)}, bf16[2,32,512]{1,2,0:T(8,128)(2,1)}, u32[]{:S(2)}, u32[]{:S(2)}) collective-permute-start(bf16[2,32,512]{1,2,0:T(8,128)(2,1)} %slice.370), channel_id=1, source_target_pairs={{0,1},{1,2},{2,3},{3,4},{4,5},{5,6},{6,7},{7,8},{8,9},{9,10},{10,1... | collective-permute-start | bytes 196616 | tf_op jit(solution)/shard_map/ppermute | solution.py:32
  355.5 3.1 copy.497
  359.3 39.8 %scatter_fusion = bf16[4,512,512]{2,0,1:T(4,128)(2,1)S(1)} fusion(bf16[4,512,512]{2,0,1:T(4,128)(2,1)S(1)} %broadcast_in_dim.142, s32[512]{0:T(512)S(1)} %copy-done.86, bf16[512,4,512]{2,1,0:T(4,128)(2,1)} %copy.497), kind=kCustom, calls=%fused_computation.1 | custom fusion | bytes 6293504 | tf_op jit(solution)/shard_map/scatter | solution.py:280
  399.0 3.1 fusion.115
  (426 shorter events, 214.5 us)
Async XLA Ops:
  33.2 84.7 %copy-start.39 = (bf16[1,32,512]{2,1,0:T(8,128)(2,1)}, bf16[1,32,512]{2,1,0:T(8,128)(2,1)S(1)}, u32[]{:S(2)}) copy-start(bf16[1,32,512]{2,1,0:T(8,128)(2,1)S(1)} %fusion.63) | copy-start | bytes 98308
  35.4 82.5 %copy-start.41 = (bf16[32,512]{1,0:T(8,128)(2,1)}, bf16[32,512]{1,0:T(8,128)(2,1)S(1)}, u32[]{:S(2)}) copy-start(bf16[32,512]{1,0:T(8,128)(2,1)S(1)} %reduce_sum.151) | copy-start | bytes 98308
  36.1 68.2 %collective-permute-start.4 = (bf16[2,32,512]{2,1,0:T(8,128)(2,1)}, bf16[2,32,512]{2,1,0:T(8,128)(2,1)}, u32[]{:S(2)}, u32[]{:S(2)}) collective-permute-start(bf16[2,32,512]{2,1,0:T(8,128)(2,1)} %pad_maximum_fusion.10), channel_id=1, source_target_pairs={{0,1},{1,2},{2,3},{3,4},{4,5},{5,6},{6,7},{7,8},{8,9},{9,10},{10,1... | collective-permute-start | bytes 196616 | tf_op jit(solution)/shard_map/ppermute | solution.py:32
  39.7 64.5 %collective-permute-start.7 = (bf16[2,32,512]{2,1,0:T(8,128)(2,1)}, bf16[2,32,512]{2,1,0:T(8,128)(2,1)S(1)}, u32[]{:S(2)}, u32[]{:S(2)}) collective-permute-start(bf16[2,32,512]{2,1,0:T(8,128)(2,1)} %pad_maximum_fusion.10), channel_id=1, source_target_pairs={{1,0},{2,1},{3,2},{4,3},{5,4},{6,5},{7,6},{8,7},{9,8},{10,9},{11,1... | collective-permute-start | bytes 196616 | tf_op jit(solution)/shard_map/ppermute | solution.py:32
  43.0 78.5 %collective-permute-start = (bf16[2,128,512]{2,0,1:T(2,128)(2,1)}, bf16[2,128,512]{2,0,1:T(2,128)(2,1)}, u32[]{:S(2)}, u32[]{:S(2)}) collective-permute-start(bf16[2,128,512]{2,0,1:T(2,128)(2,1)} %get-tuple-element.37), channel_id=1, source_target_pairs={{0,1},{1,2},{2,3},{3,4},{4,5},{5,6},{6,7},{7,8},{8,9},{9,10},{10,1... | collective-permute-start | bytes 786440 | tf_op jit(solution)/shard_map/ppermute | solution.py:21
  50.9 13.1 %copy-start.30 = (bf16[512,512]{1,0:T(8,128)(2,1)S(1)}, bf16[512,512]{1,0:T(8,128)(2,1)}, u32[]{:S(2)}) copy-start(bf16[512,512]{1,0:T(8,128)(2,1)} %get-tuple-element.35) | copy-start | bytes 1572868
  50.9 75.5 %collective-permute-start.1 = (bf16[2,128,512]{2,0,1:T(2,128)(2,1)}, bf16[2,128,512]{2,0,1:T(2,128)(2,1)}, u32[]{:S(2)}, u32[]{:S(2)}) collective-permute-start(bf16[2,128,512]{2,0,1:T(2,128)(2,1)} %get-tuple-element.38), channel_id=1, source_target_pairs={{1,0},{2,1},{3,2},{4,3},{5,4},{6,5},{7,6},{8,7},{9,8},{10,9},{11,1... | collective-permute-start | bytes 786440 | tf_op jit(solution)/shard_map/ppermute | solution.py:24
  69.4 77.0 %collective-permute-start.2 = (bf16[2,128,512]{2,1,0:T(8,128)(2,1)}, bf16[2,128,512]{2,1,0:T(8,128)(2,1)}, u32[]{:S(2)}, u32[]{:S(2)}) collective-permute-start(bf16[2,128,512]{2,1,0:T(8,128)(2,1)} %get-tuple-element.60), channel_id=1, source_target_pairs={{0,1},{1,2},{2,3},{3,4},{4,5},{5,6},{6,7},{7,8},{8,9},{9,10},{10,1... | collective-permute-start | bytes 786440 | tf_op jit(solution)/shard_map/ppermute | solution.py:21
  81.1 18.1 %copy-start.7 = (f32[1,512,512]{1,2,0:T(8,128)}, f32[1,512,512]{1,2,0:T(8,128)S(1)}, u32[]{:S(2)}) copy-start(f32[1,512,512]{1,2,0:T(8,128)S(1)} %copy.445) | copy-start | bytes 3145732
  89.4 50.0 %copy-start.9 = (bf16[4,128,8,64]{1,3,2,0:T(8,128)(2,1)}, bf16[4,128,8,64]{1,3,2,0:T(8,128)(2,1)S(1)}, u32[]{:S(2)}) copy-start(bf16[4,128,8,64]{1,3,2,0:T(8,128)(2,1)S(1)} %copy.419) | copy-start | bytes 1572868
  103.4 40.2 %copy-start.27 = (pred[4,128,384]{2,1,0:T(8,128)(4,1)}, pred[4,128,384]{2,1,0:T(8,128)(4,1)S(1)}, u32[]{:S(2)}) copy-start(pred[4,128,384]{2,1,0:T(8,128)(4,1)S(1)} %fusion.29) | copy-start | bytes 589828
  104.3 27.0 %copy-start.44 = (bf16[2,32,512]{2,1,0:T(8,128)(2,1)}, bf16[2,32,512]{2,1,0:T(8,128)(2,1)S(1)}, u32[]{:S(2)}) copy-start(bf16[2,32,512]{2,1,0:T(8,128)(2,1)S(1)} %collective-permute-done.7) | copy-start | bytes 196612
  105.2 6.0 %collective-permute-start.5 = (bf16[2,64,512]{2,1,0:T(8,128)(2,1)S(1)}, bf16[2,64,512]{2,1,0:T(8,128)(2,1)S(1)}, u32[]{:S(2)}, u32[]{:S(2)}) collective-permute-start(bf16[2,64,512]{2,1,0:T(8,128)(2,1)S(1)} %get-tuple-element.64), channel_id=1, source_target_pairs={{0,2},{1,3},{2,4},{3,5},{4,6},{5,7},{6,8},{7,9},{8,10},{9,11},{10,... | collective-permute-start | bytes 393224 | tf_op jit(solution)/shard_map/ppermute | solution.py:32
  107.1 10.8 %collective-permute-start.8 = (bf16[2,64,512]{2,1,0:T(8,128)(2,1)S(1)}, bf16[2,64,512]{2,1,0:T(8,128)(2,1)S(1)}, u32[]{:S(2)}, u32[]{:S(2)}) collective-permute-start(bf16[2,64,512]{2,1,0:T(8,128)(2,1)S(1)} %get-tuple-element.63), channel_id=1, source_target_pairs={{2,0},{3,1},{4,2},{5,3},{6,4},{7,5},{8,6},{9,7},{10,8},{11,9},{12,... | collective-permute-start | bytes 393224 | tf_op jit(solution)/shard_map/ppermute | solution.py:32
  111.2 15.3 %copy-start.48 = (bf16[2,64,512]{2,1,0:T(8,128)(2,1)}, bf16[2,64,512]{2,1,0:T(8,128)(2,1)S(1)}, u32[]{:S(2)}) copy-start(bf16[2,64,512]{2,1,0:T(8,128)(2,1)S(1)} %collective-permute-done.5) | copy-start | bytes 393220
  111.2 35.2 %collective-permute-start.3 = (bf16[2,128,512]{2,1,0:T(8,128)(2,1)}, bf16[2,128,512]{2,1,0:T(8,128)(2,1)}, u32[]{:S(2)}, u32[]{:S(2)}) collective-permute-start(bf16[2,128,512]{2,1,0:T(8,128)(2,1)} %get-tuple-element.60), channel_id=1, source_target_pairs={{1,0},{2,1},{3,2},{4,3},{5,4},{6,5},{7,6},{8,7},{9,8},{10,9},{11,1... | collective-permute-start | bytes 786440 | tf_op jit(solution)/shard_map/ppermute | solution.py:24
  119.6 67.1 %collective-permute-start.6 = (bf16[2,128,512]{2,1,0:T(8,128)(2,1)}, bf16[2,128,512]{2,1,0:T(8,128)(2,1)}, u32[]{:S(2)}, u32[]{:S(2)}) collective-permute-start(bf16[2,128,512]{2,1,0:T(8,128)(2,1)} %get-tuple-element.62), channel_id=1, source_target_pairs={{0,4},{1,5},{2,6},{3,7},{4,8},{5,9},{6,10},{7,11},{8,12},{9,13},{1... | collective-permute-start | bytes 786440 | tf_op jit(solution)/shard_map/ppermute | solution.py:32
  121.5 69.8 %collective-permute-start.9 = (bf16[2,128,512]{2,1,0:T(8,128)(2,1)}, bf16[2,128,512]{2,1,0:T(8,128)(2,1)}, u32[]{:S(2)}, u32[]{:S(2)}) collective-permute-start(bf16[2,128,512]{2,1,0:T(8,128)(2,1)} %get-tuple-element.61), channel_id=1, source_target_pairs={{4,0},{5,1},{6,2},{7,3},{8,4},{9,5},{10,6},{11,7},{12,8},{13,9},{1... | collective-permute-start | bytes 786440 | tf_op jit(solution)/shard_map/ppermute | solution.py:32
  177.0 12.5 %copy-start.40 = (bf16[1,32,512]{2,1,0:T(8,128)(2,1)S(1)}, bf16[1,32,512]{2,1,0:T(8,128)(2,1)}, u32[]{:S(2)}) copy-start(bf16[1,32,512]{2,1,0:T(8,128)(2,1)} %copy-done.39) | copy-start | bytes 98308
  177.0 12.5 %copy-start.42 = (bf16[32,512]{1,0:T(8,128)(2,1)S(1)}, bf16[32,512]{1,0:T(8,128)(2,1)}, u32[]{:S(2)}) copy-start(bf16[32,512]{1,0:T(8,128)(2,1)} %copy-done.41) | copy-start | bytes 98308
  196.7 49.4 %copy-start.57 = (f32[8,32]{1,0:T(8,128)}, f32[8,32]{1,0:T(8,128)S(1)}, u32[]{:S(2)}) copy-start(f32[8,32]{1,0:T(8,128)S(1)} %get-tuple-element.65) | copy-start | bytes 3076
  270.5 44.5 %collective-permute-start.12 = (bf16[2,128,512]{1,2,0:T(8,128)(2,1)}, bf16[2,128,512]{1,2,0:T(8,128)(2,1)}, u32[]{:S(2)}, u32[]{:S(2)}) collective-permute-start(bf16[2,128,512]{1,2,0:T(8,128)(2,1)} %get-tuple-element.51), channel_id=1, source_target_pairs={{0,1},{1,2},{2,3},{3,4},{4,5},{5,6},{6,7},{7,8},{8,9},{9,10},{10,1... | collective-permute-start | bytes 786440 | tf_op jit(solution)/shard_map/ppermute | solution.py:32
  278.3 23.3 %collective-permute-start.14 = (bf16[2,128,512]{1,2,0:T(8,128)(2,1)}, bf16[2,128,512]{1,2,0:T(8,128)(2,1)S(1)}, u32[]{:S(2)}, u32[]{:S(2)}) collective-permute-start(bf16[2,128,512]{1,2,0:T(8,128)(2,1)} %get-tuple-element.45), channel_id=1, source_target_pairs={{4,0},{5,1},{6,2},{7,3},{8,4},{9,5},{10,6},{11,7},{12,8},{13,9},{1... | collective-permute-start | bytes 786440 | tf_op jit(solution)/shard_map/ppermute | solution.py:32
  284.6 19.3 %collective-permute-start.17 = (bf16[2,128,512]{1,2,0:T(8,128)(2,1)}, bf16[2,128,512]{1,2,0:T(8,128)(2,1)}, u32[]{:S(2)}, u32[]{:S(2)}) collective-permute-start(bf16[2,128,512]{1,2,0:T(8,128)(2,1)} %get-tuple-element.46), channel_id=1, source_target_pairs={{0,4},{1,5},{2,6},{3,7},{4,8},{5,9},{6,10},{7,11},{8,12},{9,13},{1... | collective-permute-start | bytes 786440 | tf_op jit(solution)/shard_map/ppermute | solution.py:32
  294.2 13.0 %collective-permute-start.10 = (bf16[2,128,512]{1,2,0:T(8,128)(2,1)}, bf16[2,128,512]{1,2,0:T(8,128)(2,1)S(1)}, u32[]{:S(2)}, u32[]{:S(2)}) collective-permute-start(bf16[2,128,512]{1,2,0:T(8,128)(2,1)} %get-tuple-element.39), channel_id=1, source_target_pairs={{0,1},{1,2},{2,3},{3,4},{4,5},{5,6},{6,7},{7,8},{8,9},{9,10},{10,1... | collective-permute-start | bytes 786440 | tf_op jit(solution)/shard_map/ppermute | solution.py:32
  296.2 18.5 %collective-permute-start.11 = (bf16[2,128,512]{1,2,0:T(8,128)(2,1)}, bf16[2,128,512]{1,2,0:T(8,128)(2,1)S(1)}, u32[]{:S(2)}, u32[]{:S(2)}) collective-permute-start(bf16[2,128,512]{1,2,0:T(8,128)(2,1)} %get-tuple-element.40), channel_id=1, source_target_pairs={{1,0},{2,1},{3,2},{4,3},{5,4},{6,5},{7,6},{8,7},{9,8},{10,9},{11,1... | collective-permute-start | bytes 786440 | tf_op jit(solution)/shard_map/ppermute | solution.py:32
  301.6 13.2 %copy-start.8 = (f32[2,768,512]{1,2,0:T(8,128)S(1)}, f32[2,768,512]{1,2,0:T(8,128)}, u32[]{:S(2)}) copy-start(f32[2,768,512]{1,2,0:T(8,128)} %get-tuple-element.10) | copy-start | bytes 9437188
  301.6 13.5 %collective-permute-start.13 = (bf16[2,128,512]{1,2,0:T(8,128)(2,1)S(1)}, bf16[2,128,512]{1,2,0:T(8,128)(2,1)S(1)}, u32[]{:S(2)}, u32[]{:S(2)}) collective-permute-start(bf16[2,128,512]{1,2,0:T(8,128)(2,1)S(1)} %copy-done.63), channel_id=1, source_target_pairs={{1,0},{2,1},{3,2},{4,3},{5,4},{6,5},{7,6},{8,7},{9,8},{10,9},{11,1... | collective-permute-start | bytes 786440 | tf_op jit(solution)/shard_map/ppermute | solution.py:32
  303.9 14.5 %collective-permute-start.15 = (bf16[2,64,512]{1,2,0:T(8,128)(2,1)S(1)}, bf16[2,64,512]{1,2,0:T(8,128)(2,1)S(1)}, u32[]{:S(2)}, u32[]{:S(2)}) collective-permute-start(bf16[2,64,512]{1,2,0:T(8,128)(2,1)S(1)} %slice.373), channel_id=1, source_target_pairs={{2,0},{3,1},{4,2},{5,3},{6,4},{7,5},{8,6},{9,7},{10,8},{11,9},{12,... | collective-permute-start | bytes 393224 | tf_op jit(solution)/shard_map/ppermute | solution.py:32
  307.1 15.8 %collective-permute-start.18 = (bf16[2,64,512]{1,2,0:T(8,128)(2,1)S(1)}, bf16[2,64,512]{1,2,0:T(8,128)(2,1)S(1)}, u32[]{:S(2)}, u32[]{:S(2)}) collective-permute-start(bf16[2,64,512]{1,2,0:T(8,128)(2,1)S(1)} %slice.371), channel_id=1, source_target_pairs={{0,2},{1,3},{2,4},{3,5},{4,6},{5,7},{6,8},{7,9},{8,10},{9,11},{10,... | collective-permute-start | bytes 393224 | tf_op jit(solution)/shard_map/ppermute | solution.py:32
  319.4 22.4 %collective-permute-start.16 = (bf16[2,32,512]{1,2,0:T(8,128)(2,1)}, bf16[2,32,512]{1,2,0:T(8,128)(2,1)}, u32[]{:S(2)}, u32[]{:S(2)}) collective-permute-start(bf16[2,32,512]{1,2,0:T(8,128)(2,1)} %slice.372), channel_id=1, source_target_pairs={{1,0},{2,1},{3,2},{4,3},{5,4},{6,5},{7,6},{8,7},{9,8},{10,9},{11,1... | collective-permute-start | bytes 196616 | tf_op jit(solution)/shard_map/ppermute | solution.py:32
  324.0 17.9 %collective-permute-start.19 = (bf16[2,32,512]{1,2,0:T(8,128)(2,1)}, bf16[2,32,512]{1,2,0:T(8,128)(2,1)}, u32[]{:S(2)}, u32[]{:S(2)}) collective-permute-start(bf16[2,32,512]{1,2,0:T(8,128)(2,1)} %slice.370), channel_id=1, source_target_pairs={{0,1},{1,2},{2,3},{3,4},{4,5},{5,6},{6,7},{7,8},{8,9},{9,10},{10,1... | collective-permute-start | bytes 196616 | tf_op jit(solution)/shard_map/ppermute | solution.py:32
  (78 other events, 288.6 us)
where the time goes:
time: 413 us; the launch traced here: 406 us
  local copies, waits for them, and re-layouts  197 us (48%)
  other arithmetic  90 us (22%)
  starting transfers between devices  80.3 us (19%)
  matrix products  29.4 us (7%)
  waiting for transfers between devices  6.94 us (2%)
    ppermute x16, starting transfers between devices, passed_along(): lax.ppermute(value, axis, [(source, source + steps) for source in range(i...  60.7 us
    scatter x1, local copies, waits for them, and re-layouts, on_device(): placed = jnp.zeros_like(results).at[:, local].set(results)  39.8 us
    another operation x10, local copies, waits for them, and re-layouts, split_heads(): return value_rows.reshape(value_rows.shape[:-1] + (HEADS, HEAD_DIM))  24.8 us
    convert_element_type x2, other arithmetic, on_device(): upstream = split_heads(ordered[3].astype(jnp.float32))  22.2 us
    unnamed x196, local copies, waits for them, and re-layouts  19.3 us
    ppermute x2, starting transfers between devices, extended(): lax.ppermute(lax.slice_in_dim(block, block.shape[dim] - width, None, axis...  15.7 us
    another operation x6, other arithmetic  9.91 us
  transfers between devices with their start and end apart: 20, of which 2 were waited for; matrix products, arithmetic and copies ran while one was open for 34% of the time, Pallas kernels for 0%

commit v1 on v0

v1 whole, which is shorter than its diff:
```python
import functools

import jax
import jax.numpy as jnp
from jax import lax
from jax.experimental import pallas as pl
from jax.experimental.pallas import tpu as pltpu
from jax.sharding import PartitionSpec as P

HEADS = 8
HEAD_DIM = 64
FEAT = 512
BLK = 128
ROWS = 512
SCALE = HEAD_DIM**-0.5
NEG = -1e30
MESH = pl.DeviceIdType.MESH
F32 = jnp.float32
BF16 = jnp.bfloat16

POS = {1: 0, 2: 1, 0: 2, 3: 4}
LEVEL1 = 3
WINDOW = {0: 128, 1: 256, 2: 0, 3: 768, 4: 384}
OWN1 = 768 + BLK
SLOTS = 10
WIN2 = 384


def nn(a, b):
    return lax.dot_general(a, b, (((1,), (0,)), ((), ())), preferred_element_type=F32)


def nt(a, b):
    return lax.dot_general(a, b, (((1,), (1,)), ((), ())), preferred_element_type=F32)


def iota(shape, dim):
    return lax.broadcasted_iota(jnp.int32, shape, dim)


def onehot(mask):
    return jnp.where(mask, 1.0, 0.0).astype(BF16)


def parts_of(x, count):
    parts = []
    for _ in range(count):
        part = x.astype(BF16)
        parts.append(part)
        x = x - part.astype(F32)
    return parts


def spread(x, matrix, count):
    total = None
    for part in parts_of(x, count):
        term = nn(part, matrix)
        total = term if total is None else total + term
    return total


def two_heads(x):
    zero = jnp.zeros((HEAD_DIM, x.shape[1]), x.dtype)
    upper = jnp.concatenate([x[:HEAD_DIM], zero], axis=1)
    lower = jnp.concatenate([zero, x[HEAD_DIM:]], axis=1)
    return jnp.concatenate([upper, lower], axis=0)


def own_blocks(x):
    return jnp.concatenate([x[:HEAD_DIM, :BLK], x[HEAD_DIM:, BLK:]], axis=0)


def kernel(
    n,
    order_ref,
    q_ref,
    k_ref,
    v_ref,
    dz_ref,
    out_ref,
    dq_out,
    dk_out,
    dv_out,
    place,
    pool1,
    pool1t,
    pool2,
    pool2t,
    kv,
    kvt,
    kv2own,
    kv2,
    kv2t,
    qg,
    halo_qg,
    stats,
    halo_stats,
    dzt,
    weights,
    sums,
    numer,
    q2m,
    g2m,
    k2m,
    v2m,
    weights2,
    numer2,
    g2own,
    g2win,
    bias1,
    bias2,
    share,
    delta,
    mixed,
    dqt,
    dq2,
    dkv,
    nb_send,
    nb_recv,
    l2_send,
    l2_recv,
):
    me = lax.axis_index("seq")
    left = lax.rem(me + n - 1, n)
    right = lax.rem(me + 1, n)
    core = lax.rem(me, 2)
    half = lax.rem(me // 2, 2)
    base = 4 * (me // 4 - 1)
    sibling = me + 1 - 2 * core
    chips = [0, 1, 3 - half, 4, 5]
    peers = [lax.rem(base + 2 * chip + core + n, n) for chip in chips]
    far_dense = [half + 3, half + 3, 2, half, half]

    barrier = pltpu.get_barrier_semaphore()
    for device in [left, right] + peers:
        pl.semaphore_signal(barrier, inc=1, device_id=(device,), device_id_type=MESH)

    def remote(src, dst, send, recv, device):
        return pltpu.make_async_remote_copy(
            src_ref=src,
            dst_ref=dst,
            send_sem=send,
            recv_sem=recv,
            device_id=(device,),
            device_id_type=MESH,
        )

    def kv0_copy(side):
        src, dst, to = [(512, 0, right), (128, 640, left)][side]
        return remote(
            kv.at[:, pl.ds(src, BLK)], kv.at[:, pl.ds(dst, BLK)],
            nb_send.at[side, 0], nb_recv.at[side, 0], to,
        )

    def kv1_copy(side):
        dst, to = [(768, right), (1024, left)][side]
        return remote(
            kv.at[:, pl.ds(OWN1, BLK)], kv.at[:, pl.ds(dst, BLK)],
            nb_send.at[side, 1], nb_recv.at[side, 1], to,
        )

    def qg_copy(side, which):
        src, to = [(3, right), (2, left)][side]
        return remote(
            qg.at[which, pl.ds(src, 2)], halo_qg.at[side, which],
            nb_send.at[side, 2 + which], nb_recv.at[side, 2 + which], to,
        )

    def stats_copy(side):
        src, to = [(3, right), (2, left)][side]
        return remote(
            stats.at[:, pl.ds(src, 2)], halo_stats.at[side],
            nb_send.at[side, 4], nb_recv.at[side, 4], to,
        )

    def slot_rows(slot):
        return pl.ds(pl.multiple_of(32 * slot, 32), 32)

    def far_refs(phase, slot):
        if phase == 0:
            return kv2own, kv2.at[:, slot_rows(slot)]
        return g2own, g2win.at[slot_rows(slot)]

    def direct_copy(phase, j):
        slot = 2 * far_dense[j] + core
        src, dst = far_refs(phase, slot)
        return remote(src, dst, l2_send.at[phase, j], l2_recv.at[phase, slot], peers[j])

    def arrival(phase, slot):
        src, dst = far_refs(phase, slot)
        return remote(src, dst, l2_send.at[phase, 0], l2_recv.at[phase, slot], sibling)

    def relay_copy(phase, j):
        slot = 2 * j + core
        _, dst = far_refs(phase, slot)
        return remote(dst, dst, l2_send.at[phase, 5 + j], l2_recv.at[phase, slot], sibling)

    order = order_ref[...] - me * ROWS
    place[...] = onehot(iota((ROWS, ROWS), 0) == order)
    column = jnp.transpose(jnp.broadcast_to(order.astype(F32), (BLK, ROWS)))
    lane = iota((ROWS, BLK), 1).astype(F32)
    gather = jnp.concatenate(
        [jnp.where(column == lane + float(BLK * i), 1.0, 0.0).astype(BF16) for i in range(4)], axis=1
    )
    pool1[...] = onehot(iota((BLK, ROWS), 0) == (iota((BLK, ROWS), 1) >> 2))
    pool1t[...] = onehot((iota((ROWS, BLK), 0) >> 2) == iota((ROWS, BLK), 1))
    pool2[...] = onehot((iota((256, ROWS), 0) & 31) == (iota((256, ROWS), 1) >> 4))
    pool2t[...] = onehot((iota((ROWS, 256), 0) >> 4) == (iota((ROWS, 256), 1) & 31))

    kv[0, 128:640] = nn(gather, k_ref[...]).astype(BF16)
    kv[1, 128:640] = nn(gather, v_ref[...]).astype(BF16)
    pl.semaphore_wait(barrier, 7)
    for side in range(2):
        kv0_copy(side).start()
    pooled_k = nn(pool2[0:32], kv[0, 128:640])
    pooled_v = nn(pool2[0:32], kv[1, 128:640])
    kv2own[0] = (pooled_k * (1.0 / 16)).astype(BF16)
    kv2own[1] = pooled_v.astype(BF16)
    query = (nn(gather, q_ref[...]) * SCALE).astype(BF16)
    kv2own[2] = (nn(pool2[0:32], query) * (1.0 / 16)).astype(BF16)
    for j in range(5):
        direct_copy(0, j).start()
    kv[0, OWN1 : OWN1 + BLK] = (nn(pool1[...], kv[0, 128:640]) * 0.25).astype(BF16)
    kv[1, OWN1 : OWN1 + BLK] = nn(pool1[...], kv[1, 128:640]).astype(BF16)
    for side in range(2):
        kv1_copy(side).start()
    query_t = jnp.transpose(query)
    for b in range(4):
        qg[0, POS[b]] = query_t[:, BLK * b : BLK * (b + 1)]
    qg[0, LEVEL1] = (nn(query_t, pool1t[...]) * 0.25).astype(BF16)
    for side in range(2):
        qg_copy(side, 0).start()

    head_lane = (iota((FEAT, 256), 0) >> 6) == (iota((FEAT, 256), 1) >> 5)
    q2m[...] = jnp.where(head_lane, nn(query_t, pool2t[...]) * (1.0 / 16), 0.0).astype(BF16)
    kvt[0, :, 128:640] = jnp.transpose(kv[0, 128:640])
    kvt[1, :, 128:640] = jnp.transpose(kv[1, 128:640])
    dzt[...] = jnp.transpose(nn(gather, dz_ref[...]).astype(BF16))
    k2m[...] = jnp.where(
        head_lane, nn(kvt[0, :, 128:640], pool2t[...]) * (1.0 / 16), 0.0
    ).astype(BF16)
    v2m[...] = jnp.where(head_lane, nn(kvt[1, :, 128:640], pool2t[...]), 0.0).astype(BF16)

    has_left = jnp.where(me > 0, 0.0, NEG).astype(F32)
    has_right = jnp.where(me < n - 1, 0.0, NEG).astype(F32)
    key_sub = (iota((WIN2, 256), 0) >> 5) - 4
    query_sub = (iota((WIN2, 256), 1) & 127) >> 5
    apart = jnp.where(jnp.abs(key_sub - query_sub) > 1, 0.0, NEG)
    bias1[0:BLK] = apart[0:BLK] + has_left
    bias1[BLK : 2 * BLK] = apart[BLK : 2 * BLK]
    bias1[2 * BLK :] = apart[2 * BLK :] + has_right
    for slot in range(12):
        if slot < SLOTS:
            device = base + 2 * chips[slot // 2] + slot % 2
            valid = (device >= 0) & (device < n) & (jnp.abs(device - me) > 1)
            level = jnp.where(valid, 0.0, NEG).astype(F32)
        else:
            level = jnp.float32(NEG)
        bias2[32 * slot : 32 * slot + 32] = jnp.zeros((32, 256), F32) + level
    for which in range(3):
        kv2[which, 320:384] = jnp.zeros((64, FEAT), BF16)
    g2win[320:384] = jnp.zeros((64, 640), BF16)

    def lanes(pair):
        return pl.ds(pl.multiple_of(BLK * pair, BLK), BLK)

    def forward(pair, pos):
        at = lanes(pair)
        start = WINDOW[pos]
        raw = nn(kv[0, start : start + 384, at], two_heads(qg[0, pos, at, :]))
        pieces = [raw[BLK * i : BLK * (i + 1)] for i in range(3)]
        if pos == POS[0]:
            pieces[0] = pieces[0] + has_left
        if pos == POS[3]:
            pieces[2] = pieces[2] + has_right
        if pos == LEVEL1:
            pieces = [piece + bias1[BLK * i : BLK * (i + 1)] for i, piece in enumerate(pieces)]
        top = jnp.max(jnp.maximum(jnp.maximum(pieces[0], pieces[1]), pieces[2]), axis=0, keepdims=True)
        total = None
        rounded = []
        for i, piece in enumerate(pieces):
            piece = jnp.exp(piece - top)
            weights[pos, pair, BLK * i : BLK * (i + 1)] = piece
            total = piece if total is None else total + piece
            rounded.append(piece.astype(BF16))
        total = jnp.sum(total, axis=0, keepdims=True) * (4.0 if pos == LEVEL1 else 1.0)
        result = nn(kvt[1, at, start : start + 384], jnp.concatenate(rounded, axis=0))
        numer[pos, at, :] = own_blocks(result)
        for e in range(2):
            stats[0, pos, pl.ds(2 * pair + e, 1), :] = top[:, BLK * e : BLK * (e + 1)]
            sums[pos, pl.ds(2 * pair + e, 1), :] = total[:, BLK * e : BLK * (e + 1)]

    def over_pairs(body):
        def step(pair, carry):
            body(pair)
            return carry

        lax.fori_loop(0, 4, step, 0)

    def forward_inner(pair):
        forward(pair, 0)
        forward(pair, 1)

    over_pairs(forward_inner)

    for j in range(5):
        arrival(0, 2 * j + core).wait_recv()
        relay_copy(0, j).start()

    for side in range(2):
        kv0_copy(side).wait_recv()
        kv1_copy(side).wait_recv()
    for which in range(2):
        kvt[which, :, 0:128] = jnp.transpose(kv[which, 0:128])
        kvt[which, :, 640:1152] = jnp.transpose(kv[which, 640:1152])

    def forward_rim(pair):
        forward(pair, 2)
        forward(pair, 3)
        forward(pair, 4)

    over_pairs(forward_rim)

    for j in range(5):
        arrival(0, 2 * j + 1 - core).wait_recv()
    for which in range(2):
        kv2t[which] = jnp.transpose(kv2[which])
    scores = nn(kv2[0], q2m[...]) + bias2[...]
    top2 = jnp.max(scores, axis=0, keepdims=True)
    scores = jnp.exp(scores - top2)
    weights2[...] = scores
    total2 = jnp.sum(scores, axis=0, keepdims=True) * 16.0
    numer2[...] = jnp.where(head_lane, nn(kv2t[1], scores.astype(BF16)), 0.0)

    def by_block(ref):
        return jnp.concatenate([ref[POS[b]] for b in range(4)], axis=1)

    head_row = iota((HEADS, 256), 0) == (iota((HEADS, 256), 1) >> 5)

    def rows2(x):
        return jnp.where(head_row, jnp.broadcast_to(x, (HEADS, 256)), 0.0)

    tops = [
        by_block(stats.at[0]),
        spread(stats[0, LEVEL1], pool1[...], 3),
        spread(rows2(top2), pool2[...], 3),
    ]
    totals = [
        by_block(sums),
        spread(sums[LEVEL1], pool1[...], 3),
        spread(rows2(total2), pool2[...], 3),
    ]
    best = jnp.maximum(jnp.maximum(tops[0], tops[1]), tops[2])
    scales = [jnp.exp(top - best) for top in tops]
    denom = scales[0] * totals[0] + scales[1] * totals[1] + scales[2] * totals[2]
    for level in range(3):
        share[level] = scales[level] / denom

    def combine(pair):
        at = lanes(pair)
        fine = jnp.concatenate([numer[POS[b], at, :] for b in range(4)], axis=1)
        middle = spread(numer[LEVEL1, at, :], pool1[...], 2)
        coarse = spread(numer2[at, :], pool2[...], 2)
        grads = dzt[at, :].astype(F32)
        for e in range(2):
            head = 2 * pair + e
            cut = slice(HEAD_DIM * e, HEAD_DIM * (e + 1))
            to = pl.ds(pl.multiple_of(HEAD_DIM * head, HEAD_DIM), HEAD_DIM)
            parts = [share[level, pl.ds(head, 1), :] for level in range(3)]
            grad = grads[cut]
            value = parts[0] * fine[cut] + parts[1] * middle[cut] + parts[2] * coarse[cut]
            mixed[to, :] = value.astype(BF16)
            delta[pl.ds(head, 1), :] = jnp.sum(grad * value, axis=0, keepdims=True)
            own = (parts[0] * grad).astype(BF16)
            for b in range(4):
                qg[1, POS[b], to, :] = own[:, BLK * b : BLK * (b + 1)]
            qg[1, LEVEL1, to, :] = spread(parts[1] * grad, pool1t[...], 2).astype(BF16)
            pooled = spread(parts[2] * grad, pool2t[...], 2)
            keep = (iota((HEAD_DIM, 256), 1) >> 5) == head
            g2m[to, :] = jnp.where(keep, pooled, 0.0).astype(BF16)

    over_pairs(combine)

    energy = share[0] * delta[...]
    for b in range(4):
        stats[1, POS[b]] = energy[:, BLK * b : BLK * (b + 1)]
    stats[1, LEVEL1] = spread(share[1] * delta[...], pool1t[...], 3) * 4.0
    energy2 = jnp.sum(
        jnp.where(head_row, spread(share[2] * delta[...], pool2t[...], 3), 0.0), axis=0, keepdims=True
    ) * 16.0

    pick = iota((32, 256), 0) == (iota((32, 256), 1) & 31)
    g2own[:, 0:FEAT] = nt(onehot(pick), g2m[...]).astype(BF16)
    packed = None
    for i, part in enumerate(parts_of(top2, 3) + parts_of(energy2, 3)):
        chosen = jnp.where(pick, jnp.broadcast_to(part.astype(F32), (32, 256)), 0.0).astype(BF16)
        target = onehot(iota((256, BLK), 1) == (iota((256, BLK), 0) >> 5) + 8 * i)
        term = nn(chosen, target)
        packed = term if packed is None else packed + term
    g2own[:, FEAT:] = packed.astype(BF16)
    for j in range(5):
        direct_copy(1, j).start()
    for side in range(2):
        qg_copy(side, 1).start()
        stats_copy(side).start()

    def pair_row(ref, pair):
        return jnp.concatenate([ref[pl.ds(2 * pair + e, 1), :] for e in range(2)], axis=1)

    def backward(pair):
        at = lanes(pair)
        key_sum, value_sum = {}, {}
        for pos in range(5):
            start = WINDOW[pos]
            window = slice(start, start + 384)
            query_m = two_heads(qg[0, pos, at, :])
            grad_m = two_heads(qg[1, pos, at, :])
            mixing = nn(kv[1, window, at], grad_m)
            weight = weights[pos, pair]
            diff = (weight * (mixing - pair_row(stats.at[1, pos], pair))).astype(BF16)
            dqt[pos, at, :] = own_blocks(nn(kvt[0, at, window], diff))
            own = [i for i in range(3) if 128 <= start + BLK * i < 640 or start + BLK * i == OWN1]
            rows = slice(BLK * own[0], BLK * (own[-1] + 1))
            key_part = nt(diff[rows], query_m)
            value_part = nt(weight[rows].astype(BF16), grad_m)
            for i in own:
                block = (start + BLK * i - 128) // BLK if pos != LEVEL1 else 4
                cut = slice(BLK * (i - own[0]), BLK * (i - own[0] + 1))
                for held, part in ((key_sum, key_part), (value_sum, value_part)):
                    held[block] = part[cut] if block not in held else held[block] + part[cut]
        for block in range(5):
            dkv[0, BLK * block : BLK * (block + 1), at] = key_sum[block]
            dkv[1, BLK * block : BLK * (block + 1), at] = value_sum[block]

    over_pairs(backward)

    for j in range(5):
        arrival(1, 2 * j + core).wait_recv()
        relay_copy(1, j).start()

    mixing2 = nn(kv2[1], g2m[...])
    diff2 = (weights2[...] * (mixing2 - energy2)).astype(BF16)
    dq2[...] = jnp.where(head_lane, nn(kv2t[0], diff2), 0.0)

    for side in range(2):
        qg_copy(side, 0).wait_recv()
        qg_copy(side, 1).wait_recv()
        stats_copy(side).wait_recv()

    far_query = (iota((BLK, 256), 1) & 127) >> 5
    far_key = iota((BLK, 256), 0) >> 5
    far_bias = [
        jnp.where(jnp.abs(far_key - far_query + 4) > 1, 0.0, NEG) + has_left,
        jnp.where(jnp.abs(far_key - far_query - 4) > 1, 0.0, NEG) + has_right,
    ]
    for side in range(2):
        bias1[BLK * side : BLK * (side + 1)] = far_bias[side]

    def from_halo(pair):
        at = lanes(pair)
        for level in range(2):
            key_sum = []
            for side in range(2):
                which = (1 - level) if side == 0 else level
                row = (128, 512)[side] if level == 0 else OWN1
                query_m = two_heads(halo_qg[side, 0, which, at, :])
                grad_m = two_heads(halo_qg[side, 1, which, at, :])
                score = nn(kv[0, row : row + BLK, at], query_m)
                if level == 0:
                    score = score + (has_left, has_right)[side]
                else:
                    score = score + bias1[BLK * side : BLK * (side + 1)]
                weight = jnp.exp(score - pair_row(halo_stats.at[side, 0, which], pair))
                mixing = nn(kv[1, row : row + BLK, at], grad_m)
                diff = weight * (mixing - pair_row(halo_stats.at[side, 1, which], pair))
                key_part = nt(diff.astype(BF16), query_m)
                value_part = nt(weight.astype(BF16), grad_m)
                to = (row - 128) if level == 0 else 512
                dkv[0, to : to + BLK, at] += key_part
                dkv[1, to : to + BLK, at] += value_part

    over_pairs(from_halo)

    for j in range(5):
        arrival(1, 2 * j + 1 - core).wait_recv()
    far_stats = g2win[:, FEAT:]
    stat_row = iota((BLK, 256), 0)
    same_head = (stat_row & 7) == (iota((BLK, 256), 1) >> 5)
    far_top = nn(far_stats, onehot(same_head & (stat_row < 24)))
    far_energy = nn(far_stats, onehot(same_head & (stat_row >= 24) & (stat_row < 48)))
    far_scores = nn(kv2[2], k2m[...]) + bias2[...]
    far_weight = jnp.exp(far_scores - far_top)
    far_mixing = nn(g2win[:, 0:FEAT], v2m[...])
    far_diff = (far_weight * (far_mixing - far_energy)).astype(BF16)
    lane_head = (iota((256, FEAT), 0) >> 5) == (iota((256, FEAT), 1) >> 6)
    dk2 = jnp.where(lane_head, nn(jnp.transpose(far_diff), kv2[2]), 0.0)
    dv2 = jnp.where(lane_head, nn(jnp.transpose(far_weight.astype(BF16)), g2win[:, 0:FEAT]), 0.0)

    def spread_rows(matrix, x):
        high, low = parts_of(x, 2)
        return nn(matrix, high) + nn(matrix, low)

    out_ref[...] = nt(place[...], mixed[...]).astype(BF16)
    query_grad = jnp.concatenate([dqt[POS[b]] for b in range(4)], axis=1)
    query_grad = query_grad + spread(dqt[LEVEL1] * 0.25, pool1[...], 2)
    query_grad = (query_grad + spread(dq2[...] * (1.0 / 16), pool2[...], 2)) * SCALE
    dq_out[...] = nt(place[...], query_grad.astype(BF16)).astype(BF16)
    key_grad = dkv[0, 0:ROWS] + spread_rows(pool1t[...], dkv[0, ROWS:] * 0.25)
    key_grad = key_grad + spread_rows(pool2t[...], dk2 * (1.0 / 16))
    dk_out[...] = nn(place[...], key_grad.astype(BF16)).astype(BF16)
    value_grad = dkv[1, 0:ROWS] + spread_rows(pool1t[...], dkv[1, ROWS:])
    value_grad = value_grad + spread_rows(pool2t[...], dv2)
    dv_out[...] = nn(place[...], value_grad.astype(BF16)).astype(BF16)

    for side in range(2):
        kv0_copy(side).wait_send()
        kv1_copy(side).wait_send()
        qg_copy(side, 0).wait_send()
        qg_copy(side, 1).wait_send()
        stats_copy(side).wait_send()
    for phase in range(2):
        for j in range(5):
            direct_copy(phase, j).wait_send()
            relay_copy(phase, j).wait_send()


def on_device(n, query_points, key_points, value_points, cotangent, hilbert_order):
    shape = jax.ShapeDtypeStruct((ROWS, FEAT), BF16)
    scratch = [
        ((ROWS, ROWS), BF16),
        ((BLK, ROWS), BF16),
        ((ROWS, BLK), BF16),
        ((256, ROWS), BF16),
        ((ROWS, 256), BF16),
        ((2, 1152, FEAT), BF16),
        ((2, FEAT, 1152), BF16),
        ((3, 32, FEAT), BF16),
        ((3, WIN2, FEAT), BF16),
        ((2, FEAT, WIN2), BF16),
        ((2, 5, FEAT, BLK), BF16),
        ((2, 2, 2, FEAT, BLK), BF16),
        ((2, 5, HEADS, BLK), F32),
        ((2, 2, 2, HEADS, BLK), F32),
        ((FEAT, ROWS), BF16),
        ((5, 4, 384, 256), F32),
        ((5, HEADS, BLK), F32),
        ((5, FEAT, BLK), F32),
        ((FEAT, 256), BF16),
        ((FEAT, 256), BF16),
        ((FEAT, 256), BF16),
        ((FEAT, 256), BF16),
        ((WIN2, 256), F32),
        ((FEAT, 256), F32),
        ((32, 640), BF16),
        ((WIN2, 640), BF16),
        ((WIN2, 256), F32),
        ((WIN2, 256), F32),
        ((3, HEADS, ROWS), F32),
        ((HEADS, ROWS), F32),
        ((FEAT, ROWS), BF16),
        ((5, FEAT, BLK), F32),
        ((FEAT, 256), F32),
        ((2, ROWS + BLK, FEAT), F32),
    ]
    return pl.pallas_call(
        functools.partial(kernel, n),
        out_shape=(shape,) * 4,
        in_specs=[pl.BlockSpec(memory_space=pltpu.VMEM)] * 5,
        out_specs=(pl.BlockSpec(memory_space=pltpu.VMEM),) * 4,
        scratch_shapes=[pltpu.VMEM(dims, kind) for dims, kind in scratch]
        + [
            pltpu.SemaphoreType.DMA((2, 5)),
            pltpu.SemaphoreType.DMA((2, 5)),
            pltpu.SemaphoreType.DMA((2, 10)),
            pltpu.SemaphoreType.DMA((2, SLOTS)),
        ],
        compiler_params=pltpu.CompilerParams(
            collective_id=0, has_side_effects=True, vmem_limit_bytes=60 * 1024 * 1024
        ),
        cost_estimate=pl.CostEstimate(
            flops=8_000_000_000, bytes_accessed=4 * 1024 * 1024, transcendentals=2_500_000
        ),
    )(hilbert_order.reshape(1, ROWS), query_points, key_points, value_points, cotangent)


def solution(mesh):
    return jax.shard_map(
        functools.partial(on_device, mesh.shape["seq"]),
        mesh=mesh,
        in_specs=(P("seq", None),) * 4 + (P("seq"),),
        out_specs=(P("seq", None),) * 4,
        check_vma=False,
    )
```

time: 413 us -> 62.2 us (0.15)
  the two profiles are of different devices: /device:TPU:63 before, /device:TPU:0 now
where the time goes in v1:
time: 62.2 us; the launch traced here: 61.9 us
  Pallas kernels  56.1 us (90%)
  local copies, waits for them, and re-layouts  5.18 us (8%)
  between operations  0.65 us (1%)
    pallas_call x1, Pallas kernels, on_device(): pl.pallas_call(functools.partial(kernel, n), out_shape=(shape,) * 4, in_s...  56.1 us
    unnamed x10, local copies, waits for them, and re-layouts  5.18 us

profile of v1, /device:TPU:0, one launch (start us, length us, event | category | flops | bytes accessed | tf_op | source)
XLA Modules:
  0.0 61.9 jit_solution(14641312502503393413)
XLA Ops:
  0.6 56.1 %shard_map.84 = (bf16[512,512]{1,0:T(8,128)(2,1)}, bf16[512,512]{1,0:T(8,128)(2,1)}, bf16[512,512]{1,0:T(8,128)(2,1)}, bf16[512,512]{1,0:T(8,128)(2,1)}) custom-call(s32[1,512]{1,0:T(1,128)} %bitcast.1, bf16[512,512]{1,0:T(8,128)(2,1)} %q_ref.1, bf16[512,512]{1,0:T(8,128)(2,1)} %k_ref.1, bf16[512,512]{1,0:T(8,128)(2,1)} %v_ref.1, bf16[512,512]{1,0:T(8,128)(2,1)} %dz_ref.1), custom_call_target="tpu_custom_call" | custom-call | flops 8000000000 | bytes 4194304 | tf_op jit(solution)/shard_map/pallas_call | solution.py:565
  56.7 0.0 copy-start.2
  56.7 1.9 %copy.13 = bf16[512,512]{1,0:T(8,128)(2,1)} copy(bf16[512,512]{1,0:T(8,128)(2,1)} %get-tuple-element.8) | data formatting | bytes 1048576
  58.7 0.0 copy-done.2
  58.7 0.0 copy-start.1
  58.7 0.8 %copy.14 = bf16[512,512]{1,0:T(8,128)(2,1)} copy(bf16[512,512]{1,0:T(8,128)(2,1)S(1)} %copy-done.2) | data formatting | bytes 1048576
  59.5 0.4 copy-done.1
  59.9 0.0 copy-start
  59.9 0.8 %copy.15 = bf16[512,512]{1,0:T(8,128)(2,1)} copy(bf16[512,512]{1,0:T(8,128)(2,1)S(1)} %copy-done.1) | data formatting | bytes 1048576
  60.7 0.4 copy-done
  61.1 0.8 %copy.16 = bf16[512,512]{1,0:T(8,128)(2,1)} copy(bf16[512,512]{1,0:T(8,128)(2,1)S(1)} %copy-done) | data formatting | bytes 1048576
Async XLA Ops:
  56.7 1.9 %copy-start.2 = (bf16[512,512]{1,0:T(8,128)(2,1)S(1)}, bf16[512,512]{1,0:T(8,128)(2,1)}, u32[]{:S(2)}) copy-start(bf16[512,512]{1,0:T(8,128)(2,1)} %get-tuple-element.9) | copy-start | bytes 1572868
  58.7 1.2 %copy-start.1 = (bf16[512,512]{1,0:T(8,128)(2,1)S(1)}, bf16[512,512]{1,0:T(8,128)(2,1)}, u32[]{:S(2)}) copy-start(bf16[512,512]{1,0:T(8,128)(2,1)} %get-tuple-element.10) | copy-start | bytes 1572868
  59.9 1.2 %copy-start = (bf16[512,512]{1,0:T(8,128)(2,1)S(1)}, bf16[512,512]{1,0:T(8,128)(2,1)}, u32[]{:S(2)}) copy-start(bf16[512,512]{1,0:T(8,128)(2,1)} %get-tuple-element.11) | copy-start | bytes 1572868

commit v2 on v1

--- a/solution.py
+++ b/solution.py
@@ -73,15 +73,13 @@
 def kernel(
     n,
     order_ref,
-    q_ref,
-    k_ref,
-    v_ref,
-    dz_ref,
-    out_ref,
-    dq_out,
-    dk_out,
-    dv_out,
-    place,
+    q_any,
+    k_any,
+    v_any,
+    dz_any,
+    out_any,
+    inputs,
+    outputs,
     pool1,
     pool1t,
     pool2,
@@ -90,6 +88,8 @@
     kvt,
     kv2own,
     kv2,
+    q2own,
+    q2win,
     kv2t,
     qg,
     halo_qg,
@@ -111,14 +111,14 @@
     bias2,
     share,
     delta,
-    mixed,
     dqt,
-    dq2,
     dkv,
     nb_send,
     nb_recv,
     l2_send,
     l2_recv,
+    in_sem,
+    out_sem,
 ):
     me = lax.axis_index("seq")
     left = lax.rem(me + n - 1, n)
@@ -131,9 +131,28 @@
     peers = [lax.rem(base + 2 * chip + core + n, n) for chip in chips]
     far_dense = [half + 3, half + 3, 2, half, half]
 
+    has_prev = me >= 4
+    has_next = me < n - 4
+    reach = [has_prev, has_prev, me >= 0, has_next, has_next]
+    near = [me > 0, me < n - 1]
+
     barrier = pltpu.get_barrier_semaphore()
-    for device in [left, right] + peers:
+
+    def greet(device):
         pl.semaphore_signal(barrier, inc=1, device_id=(device,), device_id_type=MESH)
+
+    for device, there in zip([left, right] + peers, near + reach):
+        pl.when(there)(functools.partial(greet, device))
+    partners = sum(there.astype(jnp.int32) for there in near + reach)
+
+    def load(i):
+        return pltpu.make_async_copy((k_any, v_any, q_any, dz_any)[i], inputs.at[i], in_sem.at[i])
+
+    def store(i):
+        return pltpu.make_async_copy(outputs.at[i], out_any.at[i], out_sem.at[i])
+
+    for i in range(4):
+        load(i).start()
 
     def remote(src, dst, send, recv, device):
         return pltpu.make_async_remote_copy(
@@ -179,6 +198,8 @@
     def far_refs(phase, slot):
         if phase == 0:
             return kv2own, kv2.at[:, slot_rows(slot)]
+        if phase == 1:
+            return q2own, q2win.at[slot_rows(slot)]
         return g2own, g2win.at[slot_rows(slot)]
 
     def direct_copy(phase, j):
@@ -195,8 +216,57 @@
         _, dst = far_refs(phase, slot)
         return remote(dst, dst, l2_send.at[phase, 5 + j], l2_recv.at[phase, slot], sibling)
 
+    def send(copies):
+        for side in range(2):
+            pl.when(near[1 - side])(copies(side).start)
+
+    def receive(copies):
+        for side in range(2):
+            pl.when(near[side])(copies(side).wait_recv)
+
+    def sent(copies):
+        for side in range(2):
+            pl.when(near[1 - side])(copies(side).wait_send)
+
+    def far_send(phase):
+        for j in range(5):
+            pl.when(reach[j])(direct_copy(phase, j).start)
+
+    def far_relay(phase):
+        for j in range(5):
+            def step(j=j):
+                arrival(phase, 2 * j + core).wait_recv()
+                relay_copy(phase, j).start()
+
+            pl.when(reach[j])(step)
+
+    def far_receive(phase):
+        for j in range(5):
+            pl.when(reach[j])(arrival(phase, 2 * j + 1 - core).wait_recv)
+
+    def clear(rows):
+        for first in rows:
+            kv[:, first : first + BLK] = jnp.zeros((2, BLK, FEAT), BF16)
+
+    def clear_side(side):
+        clear(((0, 768), (640, 1024))[side])
+        halo_qg[side] = jnp.zeros((2, 2, FEAT, BLK), BF16)
+        halo_stats[side] = jnp.zeros((2, 2, HEADS, BLK), F32)
+
+    def clear_far(first):
+        kv2[:, first : first + 128] = jnp.zeros((2, 128, FEAT), BF16)
+        q2win[first : first + 128] = jnp.zeros((128, FEAT), BF16)
+        g2win[first : first + 128] = jnp.zeros((128, 640), BF16)
+
+    for side in range(2):
+        pl.when(jnp.logical_not(near[side]))(functools.partial(clear_side, side))
+    pl.when(jnp.logical_not(has_prev))(functools.partial(clear_far, 0))
+    pl.when(jnp.logical_not(has_next))(functools.partial(clear_far, 192))
+    kv2[:, 320:384] = jnp.zeros((2, 64, FEAT), BF16)
+    q2win[320:384] = jnp.zeros((64, FEAT), BF16)
+    g2win[320:384] = jnp.zeros((64, 640), BF16)
+
     order = order_ref[...] - me * ROWS
-    place[...] = onehot(iota((ROWS, ROWS), 0) == order)
     column = jnp.transpose(jnp.broadcast_to(order.astype(F32), (BLK, ROWS)))
     lane = iota((ROWS, BLK), 1).astype(F32)
     gather = jnp.concatenate(
@@ -207,35 +277,31 @@
     pool2[...] = onehot((iota((256, ROWS), 0) & 31) == (iota((256, ROWS), 1) >> 4))
     pool2t[...] = onehot((iota((ROWS, 256), 0) >> 4) == (iota((ROWS, 256), 1) & 31))
 
-    kv[0, 128:640] = nn(gather, k_ref[...]).astype(BF16)
-    kv[1, 128:640] = nn(gather, v_ref[...]).astype(BF16)
-    pl.semaphore_wait(barrier, 7)
-    for side in range(2):
-        kv0_copy(side).start()
-    pooled_k = nn(pool2[0:32], kv[0, 128:640])
-    pooled_v = nn(pool2[0:32], kv[1, 128:640])
-    kv2own[0] = (pooled_k * (1.0 / 16)).astype(BF16)
-    kv2own[1] = pooled_v.astype(BF16)
-    query = (nn(gather, q_ref[...]) * SCALE).astype(BF16)
-    kv2own[2] = (nn(pool2[0:32], query) * (1.0 / 16)).astype(BF16)
-    for j in range(5):
-        direct_copy(0, j).start()
+    for which in range(2):
+        load(which).wait()
+        kv[which, 128:640] = nn(gather, inputs[which]).astype(BF16)
+    pl.semaphore_wait(barrier, partners)
+    send(kv0_copy)
     kv[0, OWN1 : OWN1 + BLK] = (nn(pool1[...], kv[0, 128:640]) * 0.25).astype(BF16)
     kv[1, OWN1 : OWN1 + BLK] = nn(pool1[...], kv[1, 128:640]).astype(BF16)
-    for side in range(2):
-        kv1_copy(side).start()
+    send(kv1_copy)
+    kv2own[0] = (nn(pool2[0:32], kv[0, 128:640]) * (1.0 / 16)).astype(BF16)
+    kv2own[1] = nn(pool2[0:32], kv[1, 128:640]).astype(BF16)
+    far_send(0)
+    load(2).wait()
+    query = (nn(gather, inputs[2]) * SCALE).astype(BF16)
+    q2own[...] = (nn(pool2[0:32], query) * (1.0 / 16)).astype(BF16)
     query_t = jnp.transpose(query)
     for b in range(4):
         qg[0, POS[b]] = query_t[:, BLK * b : BLK * (b + 1)]
     qg[0, LEVEL1] = (nn(query_t, pool1t[...]) * 0.25).astype(BF16)
-    for side in range(2):
-        qg_copy(side, 0).start()
 
     head_lane = (iota((FEAT, 256), 0) >> 6) == (iota((FEAT, 256), 1) >> 5)
     q2m[...] = jnp.where(head_lane, nn(query_t, pool2t[...]) * (1.0 / 16), 0.0).astype(BF16)
     kvt[0, :, 128:640] = jnp.transpose(kv[0, 128:640])
     kvt[1, :, 128:640] = jnp.transpose(kv[1, 128:640])
-    dzt[...] = jnp.transpose(nn(gather, dz_ref[...]).astype(BF16))
+    load(3).wait()
+    dzt[...] = jnp.transpose(nn(gather, inputs[3]).astype(BF16))
     k2m[...] = jnp.where(
         head_lane, nn(kvt[0, :, 128:640], pool2t[...]) * (1.0 / 16), 0.0
     ).astype(BF16)
@@ -257,9 +323,6 @@
         else:
             level = jnp.float32(NEG)
         bias2[32 * slot : 32 * slot + 32] = jnp.zeros((32, 256), F32) + level
-    for which in range(3):
-        kv2[which, 320:384] = jnp.zeros((64, FEAT), BF16)
-    g2win[320:384] = jnp.zeros((64, 640), BF16)
 
     def lanes(pair):
         return pl.ds(pl.multiple_of(BLK * pair, BLK), BLK)
@@ -303,13 +366,11 @@
 
     over_pairs(forward_inner)
 
-    for j in range(5):
-        arrival(0, 2 * j + core).wait_recv()
-        relay_copy(0, j).start()
-
-    for side in range(2):
-        kv0_copy(side).wait_recv()
-        kv1_copy(side).wait_recv()
+    receive(kv0_copy)
+    receive(kv1_copy)
+    send(lambda side: qg_copy(side, 0))
+    far_relay(0)
+    far_send(1)
     for which in range(2):
         kvt[which, :, 0:128] = jnp.transpose(kv[which, 0:128])
         kvt[which, :, 640:1152] = jnp.transpose(kv[which, 640:1152])
@@ -321,8 +382,7 @@
 
     over_pairs(forward_rim)
 
-    for j in range(5):
-        arrival(0, 2 * j + 1 - core).wait_recv()
+    far_receive(0)
     for which in range(2):
         kv2t[which] = jnp.transpose(kv2[which])
     scores = nn(kv2[0], q2m[...]) + bias2[...]
@@ -369,7 +429,7 @@
             parts = [share[level, pl.ds(head, 1), :] for level in range(3)]
             grad = grads[cut]
             value = parts[0] * fine[cut] + parts[1] * middle[cut] + parts[2] * coarse[cut]
-            mixed[to, :] = value.astype(BF16)
+            outputs[0, to, :] = value.astype(BF16)
             delta[pl.ds(head, 1), :] = jnp.sum(grad * value, axis=0, keepdims=True)
             own = (parts[0] * grad).astype(BF16)
             for b in range(4):
@@ -380,6 +440,7 @@
             g2m[to, :] = jnp.where(keep, pooled, 0.0).astype(BF16)
 
     over_pairs(combine)
+    store(0).start()
 
     energy = share[0] * delta[...]
     for b in range(4):
@@ -398,11 +459,9 @@
         term = nn(chosen, target)
         packed = term if packed is None else packed + term
     g2own[:, FEAT:] = packed.astype(BF16)
-    for j in range(5):
-        direct_copy(1, j).start()
-    for side in range(2):
-        qg_copy(side, 1).start()
-        stats_copy(side).start()
+    send(stats_copy)
+    send(lambda side: qg_copy(side, 1))
+    far_send(2)
 
     def pair_row(ref, pair):
         return jnp.concatenate([ref[pl.ds(2 * pair + e, 1), :] for e in range(2)], axis=1)
@@ -434,18 +493,21 @@
 
     over_pairs(backward)
 
-    for j in range(5):
-        arrival(1, 2 * j + core).wait_recv()
-        relay_copy(1, j).start()
+    far_relay(1)
+    far_relay(2)
 
     mixing2 = nn(kv2[1], g2m[...])
     diff2 = (weights2[...] * (mixing2 - energy2)).astype(BF16)
-    dq2[...] = jnp.where(head_lane, nn(kv2t[0], diff2), 0.0)
-
-    for side in range(2):
-        qg_copy(side, 0).wait_recv()
-        qg_copy(side, 1).wait_recv()
-        stats_copy(side).wait_recv()
+    dq2 = jnp.where(head_lane, nn(kv2t[0], diff2), 0.0)
+    query_grad = jnp.concatenate([dqt[POS[b]] for b in range(4)], axis=1)
+    query_grad = query_grad + spread(dqt[LEVEL1] * 0.25, pool1[...], 2)
+    query_grad = (query_grad + spread(dq2 * (1.0 / 16), pool2[...], 2)) * SCALE
+    outputs[1] = query_grad.astype(BF16)
+    store(1).start()
+
+    receive(lambda side: qg_copy(side, 0))
+    receive(stats_copy)
+    receive(lambda side: qg_copy(side, 1))
 
     far_query = (iota((BLK, 256), 1) & 127) >> 5
     far_key = iota((BLK, 256), 0) >> 5
@@ -481,61 +543,81 @@
 
     over_pairs(from_halo)
 
-    for j in range(5):
-        arrival(1, 2 * j + 1 - core).wait_recv()
+    far_receive(1)
+    far_receive(2)
     far_stats = g2win[:, FEAT:]
     stat_row = iota((BLK, 256), 0)
     same_head = (stat_row & 7) == (iota((BLK, 256), 1) >> 5)
     far_top = nn(far_stats, onehot(same_head & (stat_row < 24)))
     far_energy = nn(far_stats, onehot(same_head & (stat_row >= 24) & (stat_row < 48)))
-    far_scores = nn(kv2[2], k2m[...]) + bias2[...]
+    far_scores = nn(q2win[...], k2m[...]) + bias2[...]
     far_weight = jnp.exp(far_scores - far_top)
     far_mixing = nn(g2win[:, 0:FEAT], v2m[...])
     far_diff = (far_weight * (far_mixing - far_energy)).astype(BF16)
     lane_head = (iota((256, FEAT), 0) >> 5) == (iota((256, FEAT), 1) >> 6)
-    dk2 = jnp.where(lane_head, nn(jnp.transpose(far_diff), kv2[2]), 0.0)
+    dk2 = jnp.where(lane_head, nn(jnp.transpose(far_diff), q2win[...]), 0.0)
     dv2 = jnp.where(lane_head, nn(jnp.transpose(far_weight.astype(BF16)), g2win[:, 0:FEAT]), 0.0)
 
     def spread_rows(matrix, x):
         high, low = parts_of(x, 2)
         return nn(matrix, high) + nn(matrix, low)
 
-    out_ref[...] = nt(place[...], mixed[...]).astype(BF16)
-    query_grad = jnp.concatenate([dqt[POS[b]] for b in range(4)], axis=1)
-    query_grad = query_grad + spread(dqt[LEVEL1] * 0.25, pool1[...], 2)
-    query_grad = (query_grad + spread(dq2[...] * (1.0 / 16), pool2[...], 2)) * SCALE
-    dq_out[...] = nt(place[...], query_grad.astype(BF16)).astype(BF16)
     key_grad = dkv[0, 0:ROWS] + spread_rows(pool1t[...], dkv[0, ROWS:] * 0.25)
     key_grad = key_grad + spread_rows(pool2t[...], dk2 * (1.0 / 16))
-    dk_out[...] = nn(place[...], key_grad.astype(BF16)).astype(BF16)
+    outputs[2] = key_grad.astype(BF16)
+    store(2).start()
     value_grad = dkv[1, 0:ROWS] + spread_rows(pool1t[...], dkv[1, ROWS:])
     value_grad = value_grad + spread_rows(pool2t[...], dv2)
-    dv_out[...] = nn(place[...], value_grad.astype(BF16)).astype(BF16)
-
-    for side in range(2):
-        kv0_copy(side).wait_send()
-        kv1_copy(side).wait_send()
-        qg_copy(side, 0).wait_send()
-        qg_copy(side, 1).wait_send()
-        stats_copy(side).wait_send()
-    for phase in range(2):
+    outputs[3] = value_grad.astype(BF16)
+    store(3).start()
+
+    for copies in (kv0_copy, kv1_copy, lambda side: qg_copy(side, 0), lambda side: qg_copy(side, 1), stats_copy):
+        sent(copies)
+    for phase in range(3):
         for j in range(5):
-            direct_copy(phase, j).wait_send()
-            relay_copy(phase, j).wait_send()
+            pl.when(reach[j])(direct_copy(phase, j).wait_send)
+            pl.when(reach[j])(relay_copy(phase, j).wait_send)
+    for i in range(4):
+        store(i).wait()
+
+
+def placing(order_ref, held_any, out_ref, dq_ref, dk_ref, dv_ref, held, results, in_sem, out_sem):
+    targets = (out_ref, dq_ref, dk_ref, dv_ref)
+
+    def load(i):
+        return pltpu.make_async_copy(held_any.at[i], held.at[i], in_sem.at[i])
+
+    def store(i):
+        return pltpu.make_async_copy(results.at[i], targets[i], out_sem.at[i])
+
+    for i in range(4):
+        load(i).start()
+    order = order_ref[...] - lax.axis_index("seq") * ROWS
+    place = onehot(iota((ROWS, ROWS), 0) == order)
+    for i in range(4):
+        load(i).wait()
+        product = nt if i < 2 else nn
+        results[i] = product(place, held[i]).astype(BF16)
+        store(i).start()
+    for i in range(4):
+        store(i).wait()
 
 
 def on_device(n, query_points, key_points, value_points, cotangent, hilbert_order):
     shape = jax.ShapeDtypeStruct((ROWS, FEAT), BF16)
     scratch = [
-        ((ROWS, ROWS), BF16),
+        ((4, ROWS, FEAT), BF16),
+        ((4, ROWS, FEAT), BF16),
         ((BLK, ROWS), BF16),
         ((ROWS, BLK), BF16),
         ((256, ROWS), BF16),
         ((ROWS, 256), BF16),
         ((2, 1152, FEAT), BF16),
         ((2, FEAT, 1152), BF16),
-        ((3, 32, FEAT), BF16),
-        ((3, WIN2, FEAT), BF16),
+        ((2, 32, FEAT), BF16),
+        ((2, WIN2, FEAT), BF16),
+        ((32, FEAT), BF16),
+        ((WIN2, FEAT), BF16),
         ((2, FEAT, WIN2), BF16),
         ((2, 5, FEAT, BLK), BF16),
         ((2, 2, 2, FEAT, BLK), BF16),
@@ -557,30 +639,43 @@
         ((WIN2, 256), F32),
         ((3, HEADS, ROWS), F32),
         ((HEADS, ROWS), F32),
-        ((FEAT, ROWS), BF16),
         ((5, FEAT, BLK), F32),
-        ((FEAT, 256), F32),
         ((2, ROWS + BLK, FEAT), F32),
     ]
-    return pl.pallas_call(
+    anywhere = pl.BlockSpec(memory_space=pl.ANY)
+    order = hilbert_order.reshape(1, ROWS)
+    held = pl.pallas_call(
         functools.partial(kernel, n),
-        out_shape=(shape,) * 4,
-        in_specs=[pl.BlockSpec(memory_space=pltpu.VMEM)] * 5,
-        out_specs=(pl.BlockSpec(memory_space=pltpu.VMEM),) * 4,
+        out_shape=jax.ShapeDtypeStruct((4, ROWS, FEAT), BF16),
+        in_specs=[pl.BlockSpec(memory_space=pltpu.VMEM)] + [pl.BlockSpec(memory_space=pltpu.HBM)] * 4,
+        out_specs=anywhere,
         scratch_shapes=[pltpu.VMEM(dims, kind) for dims, kind in scratch]
         + [
             pltpu.SemaphoreType.DMA((2, 5)),
             pltpu.SemaphoreType.DMA((2, 5)),
-            pltpu.SemaphoreType.DMA((2, 10)),
-            pltpu.SemaphoreType.DMA((2, SLOTS)),
+            pltpu.SemaphoreType.DMA((3, 10)),
+            pltpu.SemaphoreType.DMA((3, SLOTS)),
+            pltpu.SemaphoreType.DMA((4,)),
+            pltpu.SemaphoreType.DMA((4,)),
         ],
         compiler_params=pltpu.CompilerParams(
-            collective_id=0, has_side_effects=True, vmem_limit_bytes=60 * 1024 * 1024
+            collective_id=0, has_side_effects=True, vmem_limit_bytes=48 * 1024 * 1024
         ),
         cost_estimate=pl.CostEstimate(
             flops=8_000_000_000, bytes_accessed=4 * 1024 * 1024, transcendentals=2_500_000
         ),
-    )(hilbert_order.reshape(1, ROWS), query_points, key_points, value_points, cotangent)
+    )(order, *[pltpu.with_memory_space_constraint(x, pltpu.HBM) for x in (query_points, key_points, value_points, cotangent)])
+    return pl.pallas_call(
+        placing,
+        out_shape=(shape,) * 4,
+        in_specs=[pl.BlockSpec(memory_space=pltpu.VMEM), anywhere],
+        out_specs=(anywhere,) * 4,
+        scratch_shapes=[pltpu.VMEM((4, ROWS, FEAT), BF16)] * 2 + [pltpu.SemaphoreType.DMA((4,))] * 2,
+        compiler_params=pltpu.CompilerParams(vmem_limit_bytes=16 * 1024 * 1024),
+        cost_estimate=pl.CostEstimate(
+            flops=1_100_000_000, bytes_accessed=4 * 1024 * 1024, transcendentals=0
+        ),
+    )(order, held)
 
 
 def solution(mesh):

time: 62.2 us -> 49.8 us (0.80)
  the two profiles are of different devices: /device:TPU:0 before, /device:TPU:97 now
where the time goes in v2:
time: 49.8 us; the launch traced here: 49.3 us
  Pallas kernels  48 us (96%)
  local copies, waits for them, and re-layouts  0.67 us (1%)
  between operations  0.65 us (1%)
    pallas_call x1, Pallas kernels, on_device(): pl.pallas_call(functools.partial(kernel, n), out_shape=jax.ShapeDtypeStru...  45 us
    pallas_call x1, Pallas kernels, on_device(): pl.pallas_call(placing, out_shape=(shape,) * 4, in_specs=[pl.BlockSpec(me...  2.95 us

profile of v2, /device:TPU:97, one launch (start us, length us, event | category | flops | bytes accessed | tf_op | source)
XLA Modules:
  0.0 49.3 jit_solution(10676946875408049113)
XLA Ops:
  0.6 0.0 copy-start
  0.6 0.7 %copy-done = s32[512]{0:T(512)S(1)} copy-done((s32[512]{0:T(512)S(1)}, s32[512]{0:T(512)}, u32[]{:S(2)}) %copy-start) | copy-done | bytes 2072
  1.3 45.0 %shard_map.84.held_any = bf16[4,512,512]{2,1,0:T(8,128)(2,1)S(1)} custom-call(s32[1,512]{1,0:T(1,128)S(1)} %bitcast.1, bf16[512,512]{1,0:T(8,128)(2,1)} %q_any.1, bf16[512,512]{1,0:T(8,128)(2,1)} %k_any.1, bf16[512,512]{1,0:T(8,128)(2,1)} %v_any.1, bf16[512,512]{1,0:T(8,128)(2,1)} %dz_any.1), custom_call_target="tpu_custom_call" | custom-call | flops 8000000000 | bytes 4194304 | tf_op jit(solution)/shard_map/pallas_call | solution.py:647
  46.3 3.0 %shard_map.85 = (bf16[512,512]{1,0:T(8,128)(2,1)}, bf16[512,512]{1,0:T(8,128)(2,1)}, bf16[512,512]{1,0:T(8,128)(2,1)}, bf16[512,512]{1,0:T(8,128)(2,1)}) custom-call(s32[1,512]{1,0:T(1,128)S(1)} %bitcast.2, bf16[4,512,512]{2,1,0:T(8,128)(2,1)S(1)} %shard_map.84.held_any), custom_call_target="tpu_custom_call" | custom-call | flops 1100000000 | bytes 4194304 | tf_op jit(solution)/shard_map/pallas_call | solution.py:668
Async XLA Ops:
  0.6 0.7 %copy-start = (s32[512]{0:T(512)S(1)}, s32[512]{0:T(512)}, u32[]{:S(2)}) copy-start(s32[512]{0:T(512)} %param.9) | copy-start | bytes 6148

commit v3 on v2

--- a/solution.py
+++ b/solution.py
@@ -72,12 +72,13 @@
 
 def kernel(
     n,
-    order_ref,
+    order_any,
     q_any,
     k_any,
     v_any,
     dz_any,
     out_any,
+    order_ref,
     inputs,
     outputs,
     pool1,
@@ -151,6 +152,8 @@
     def store(i):
         return pltpu.make_async_copy(outputs.at[i], out_any.at[i], out_sem.at[i])
 
+    order_load = pltpu.make_async_copy(order_any, order_ref, in_sem.at[4])
+    order_load.start()
     for i in range(4):
         load(i).start()
 
@@ -266,6 +269,7 @@
     q2win[320:384] = jnp.zeros((64, FEAT), BF16)
     g2win[320:384] = jnp.zeros((64, 640), BF16)
 
+    order_load.wait()
     order = order_ref[...] - me * ROWS
     column = jnp.transpose(jnp.broadcast_to(order.astype(F32), (BLK, ROWS)))
     lane = iota((ROWS, BLK), 1).astype(F32)
@@ -325,12 +329,17 @@
         bias2[32 * slot : 32 * slot + 32] = jnp.zeros((32, 256), F32) + level
 
     def lanes(pair):
-        return pl.ds(pl.multiple_of(BLK * pair, BLK), BLK)
-
-    def forward(pair, pos):
+        return slice(BLK * pair, BLK * (pair + 1))
+
+    def head_rows(head):
+        return slice(HEAD_DIM * head, HEAD_DIM * (head + 1))
+
+    def forward_scores(pair, pos):
         at = lanes(pair)
         start = WINDOW[pos]
-        raw = nn(kv[0, start : start + 384, at], two_heads(qg[0, pos, at, :]))
+        return nn(kv[0, start : start + 384, at], two_heads(qg[0, pos, at, :]))
+
+    def forward_weights(pair, pos, raw):
         pieces = [raw[BLK * i : BLK * (i + 1)] for i in range(3)]
         if pos == POS[0]:
             pieces[0] = pieces[0] + has_left
@@ -347,24 +356,26 @@
             total = piece if total is None else total + piece
             rounded.append(piece.astype(BF16))
         total = jnp.sum(total, axis=0, keepdims=True) * (4.0 if pos == LEVEL1 else 1.0)
-        result = nn(kvt[1, at, start : start + 384], jnp.concatenate(rounded, axis=0))
-        numer[pos, at, :] = own_blocks(result)
         for e in range(2):
             stats[0, pos, pl.ds(2 * pair + e, 1), :] = top[:, BLK * e : BLK * (e + 1)]
             sums[pos, pl.ds(2 * pair + e, 1), :] = total[:, BLK * e : BLK * (e + 1)]
-
-    def over_pairs(body):
-        def step(pair, carry):
-            body(pair)
-            return carry
-
-        lax.fori_loop(0, 4, step, 0)
-
-    def forward_inner(pair):
-        forward(pair, 0)
-        forward(pair, 1)
-
-    over_pairs(forward_inner)
+        return jnp.concatenate(rounded, axis=0)
+
+    def forward_mix(pair, pos, rounded):
+        at = lanes(pair)
+        start = WINDOW[pos]
+        numer[pos, at, :] = own_blocks(nn(kvt[1, at, start : start + 384], rounded))
+
+    def forward_all(units):
+        raws = [forward_scores(*unit) for unit in units]
+        rounded = [forward_weights(*unit, raw) for unit, raw in zip(units, raws)]
+        for unit, value in zip(units, rounded):
+            forward_mix(*unit, value)
+
+    def forward_inner(pairs):
+        forward_all([(pair, pos) for pair in pairs for pos in (0, 1)])
+
+    forward_inner(range(4))
 
     receive(kv0_copy)
     receive(kv1_copy)
@@ -375,12 +386,10 @@
         kvt[which, :, 0:128] = jnp.transpose(kv[which, 0:128])
         kvt[which, :, 640:1152] = jnp.transpose(kv[which, 640:1152])
 
-    def forward_rim(pair):
-        forward(pair, 2)
-        forward(pair, 3)
-        forward(pair, 4)
-
-    over_pairs(forward_rim)
+    def forward_rim(pairs):
+        forward_all([(pair, pos) for pair in pairs for pos in (2, 4, 3)])
+
+    forward_rim(range(4))
 
     far_receive(0)
     for which in range(2):
@@ -416,30 +425,37 @@
     for level in range(3):
         share[level] = scales[level] / denom
 
-    def combine(pair):
-        at = lanes(pair)
-        fine = jnp.concatenate([numer[POS[b], at, :] for b in range(4)], axis=1)
-        middle = spread(numer[LEVEL1, at, :], pool1[...], 2)
-        coarse = spread(numer2[at, :], pool2[...], 2)
-        grads = dzt[at, :].astype(F32)
-        for e in range(2):
-            head = 2 * pair + e
-            cut = slice(HEAD_DIM * e, HEAD_DIM * (e + 1))
-            to = pl.ds(pl.multiple_of(HEAD_DIM * head, HEAD_DIM), HEAD_DIM)
-            parts = [share[level, pl.ds(head, 1), :] for level in range(3)]
-            grad = grads[cut]
-            value = parts[0] * fine[cut] + parts[1] * middle[cut] + parts[2] * coarse[cut]
-            outputs[0, to, :] = value.astype(BF16)
-            delta[pl.ds(head, 1), :] = jnp.sum(grad * value, axis=0, keepdims=True)
-            own = (parts[0] * grad).astype(BF16)
-            for b in range(4):
-                qg[1, POS[b], to, :] = own[:, BLK * b : BLK * (b + 1)]
-            qg[1, LEVEL1, to, :] = spread(parts[1] * grad, pool1t[...], 2).astype(BF16)
-            pooled = spread(parts[2] * grad, pool2t[...], 2)
+    def combine(pairs):
+        spreads = []
+        for pair in pairs:
+            at = lanes(pair)
+            spreads.append((spread(numer[LEVEL1, at, :], pool1[...], 2), spread(numer2[at, :], pool2[...], 2)))
+        scaled = []
+        for pair, (middle, coarse) in zip(pairs, spreads):
+            at = lanes(pair)
+            fine = jnp.concatenate([numer[POS[b], at, :] for b in range(4)], axis=1)
+            grads = dzt[at, :].astype(F32)
+            for e in range(2):
+                head = 2 * pair + e
+                cut = slice(HEAD_DIM * e, HEAD_DIM * (e + 1))
+                to = head_rows(head)
+                parts = [share[level, pl.ds(head, 1), :] for level in range(3)]
+                grad = grads[cut]
+                value = parts[0] * fine[cut] + parts[1] * middle[cut] + parts[2] * coarse[cut]
+                outputs[0, to, :] = value.astype(BF16)
+                delta[pl.ds(head, 1), :] = jnp.sum(grad * value, axis=0, keepdims=True)
+                own = (parts[0] * grad).astype(BF16)
+                for b in range(4):
+                    qg[1, POS[b], to, :] = own[:, BLK * b : BLK * (b + 1)]
+                scaled.append((head, parts_of(parts[1] * grad, 2), parts_of(parts[2] * grad, 2)))
+        for head, middle, coarse in scaled:
+            to = head_rows(head)
+            qg[1, LEVEL1, to, :] = (nn(middle[0], pool1t[...]) + nn(middle[1], pool1t[...])).astype(BF16)
+            pooled = nn(coarse[0], pool2t[...]) + nn(coarse[1], pool2t[...])
             keep = (iota((HEAD_DIM, 256), 1) >> 5) == head
             g2m[to, :] = jnp.where(keep, pooled, 0.0).astype(BF16)
 
-    over_pairs(combine)
+    combine(range(4))
     store(0).start()
 
     energy = share[0] * delta[...]
@@ -466,32 +482,44 @@
     def pair_row(ref, pair):
         return jnp.concatenate([ref[pl.ds(2 * pair + e, 1), :] for e in range(2)], axis=1)
 
-    def backward(pair):
-        at = lanes(pair)
-        key_sum, value_sum = {}, {}
-        for pos in range(5):
+    def backward(pairs):
+        sums_of = [({}, {}) for pair in pairs]
+
+        def mixing_of(pair, pos):
+            at = lanes(pair)
             start = WINDOW[pos]
-            window = slice(start, start + 384)
+            return nn(kv[1, start : start + 384, at], two_heads(qg[1, pos, at, :]))
+
+        def diff_of(pair, pos, mixing):
+            return (weights[pos, pair] * (mixing - pair_row(stats.at[1, pos], pair))).astype(BF16)
+
+        def grads_of(sums_here, pair, pos, diff):
+            at = lanes(pair)
+            start = WINDOW[pos]
             query_m = two_heads(qg[0, pos, at, :])
             grad_m = two_heads(qg[1, pos, at, :])
-            mixing = nn(kv[1, window, at], grad_m)
-            weight = weights[pos, pair]
-            diff = (weight * (mixing - pair_row(stats.at[1, pos], pair))).astype(BF16)
-            dqt[pos, at, :] = own_blocks(nn(kvt[0, at, window], diff))
+            dqt[pos, at, :] = own_blocks(nn(kvt[0, at, start : start + 384], diff))
             own = [i for i in range(3) if 128 <= start + BLK * i < 640 or start + BLK * i == OWN1]
             rows = slice(BLK * own[0], BLK * (own[-1] + 1))
             key_part = nt(diff[rows], query_m)
-            value_part = nt(weight[rows].astype(BF16), grad_m)
+            value_part = nt(weights[pos, pair, rows].astype(BF16), grad_m)
             for i in own:
                 block = (start + BLK * i - 128) // BLK if pos != LEVEL1 else 4
                 cut = slice(BLK * (i - own[0]), BLK * (i - own[0] + 1))
-                for held, part in ((key_sum, key_part), (value_sum, value_part)):
+                for held, part in zip(sums_here, (key_part, value_part)):
                     held[block] = part[cut] if block not in held else held[block] + part[cut]
-        for block in range(5):
-            dkv[0, BLK * block : BLK * (block + 1), at] = key_sum[block]
-            dkv[1, BLK * block : BLK * (block + 1), at] = value_sum[block]
-
-    over_pairs(backward)
+            if pos == 4:
+                for which in range(2):
+                    for block in range(5):
+                        dkv[which, BLK * block : BLK * (block + 1), at] = sums_here[which][block]
+
+        units = [(pair, pos) for pair in pairs for pos in range(5)]
+        mixings = [mixing_of(*unit) for unit in units]
+        diffs = [diff_of(*unit, mixing) for unit, mixing in zip(units, mixings)]
+        for i, (unit, diff) in enumerate(zip(units, diffs)):
+            grads_of(sums_of[i // 5], *unit, diff)
+
+    backward(range(4))
 
     far_relay(1)
     far_relay(2)
@@ -518,30 +546,47 @@
     for side in range(2):
         bias1[BLK * side : BLK * (side + 1)] = far_bias[side]
 
-    def from_halo(pair):
-        at = lanes(pair)
-        for level in range(2):
-            key_sum = []
-            for side in range(2):
-                which = (1 - level) if side == 0 else level
-                row = (128, 512)[side] if level == 0 else OWN1
-                query_m = two_heads(halo_qg[side, 0, which, at, :])
-                grad_m = two_heads(halo_qg[side, 1, which, at, :])
-                score = nn(kv[0, row : row + BLK, at], query_m)
-                if level == 0:
-                    score = score + (has_left, has_right)[side]
-                else:
-                    score = score + bias1[BLK * side : BLK * (side + 1)]
-                weight = jnp.exp(score - pair_row(halo_stats.at[side, 0, which], pair))
-                mixing = nn(kv[1, row : row + BLK, at], grad_m)
-                diff = weight * (mixing - pair_row(halo_stats.at[side, 1, which], pair))
-                key_part = nt(diff.astype(BF16), query_m)
-                value_part = nt(weight.astype(BF16), grad_m)
-                to = (row - 128) if level == 0 else 512
-                dkv[0, to : to + BLK, at] += key_part
-                dkv[1, to : to + BLK, at] += value_part
-
-    over_pairs(from_halo)
+    def from_halo(pairs):
+        units = [(pair, level, side) for pair in pairs for level in range(2) for side in range(2)]
+
+        def place_of(level, side):
+            which = (1 - level) if side == 0 else level
+            return which, ((128, 512)[side] if level == 0 else OWN1)
+
+        scores, mixings = [], []
+        for pair, level, side in units:
+            which, row = place_of(level, side)
+            at = lanes(pair)
+            scores.append(nn(kv[0, row : row + BLK, at], two_heads(halo_qg[side, 0, which, at, :])))
+            mixings.append(nn(kv[1, row : row + BLK, at], two_heads(halo_qg[side, 1, which, at, :])))
+        pieces = []
+        for (pair, level, side), score, mixing in zip(units, scores, mixings):
+            which, row = place_of(level, side)
+            if level == 0:
+                score = score + (has_left, has_right)[side]
+            else:
+                score = score + bias1[BLK * side : BLK * (side + 1)]
+            weight = jnp.exp(score - pair_row(halo_stats.at[side, 0, which], pair))
+            diff = weight * (mixing - pair_row(halo_stats.at[side, 1, which], pair))
+            pieces.append((weight.astype(BF16), diff.astype(BF16)))
+        parts = []
+        for (pair, level, side), (weight, diff) in zip(units, pieces):
+            which, row = place_of(level, side)
+            at = lanes(pair)
+            parts.append(
+                (
+                    nt(diff, two_heads(halo_qg[side, 0, which, at, :])),
+                    nt(weight, two_heads(halo_qg[side, 1, which, at, :])),
+                )
+            )
+        for (pair, level, side), both in zip(units, parts):
+            which, row = place_of(level, side)
+            at = lanes(pair)
+            to = (row - 128) if level == 0 else 512
+            for i in range(2):
+                dkv[i, to : to + BLK, at] += both[i]
+
+    from_halo(range(4))
 
     far_receive(1)
     far_receive(2)
@@ -581,7 +626,7 @@
         store(i).wait()
 
 
-def placing(order_ref, held_any, out_ref, dq_ref, dk_ref, dv_ref, held, results, in_sem, out_sem):
+def placing(order_any, held_any, out_ref, dq_ref, dk_ref, dv_ref, order_ref, held, results, in_sem, out_sem):
     targets = (out_ref, dq_ref, dk_ref, dv_ref)
 
     def load(i):
@@ -590,8 +635,11 @@
     def store(i):
         return pltpu.make_async_copy(results.at[i], targets[i], out_sem.at[i])
 
+    order_load = pltpu.make_async_copy(order_any, order_ref, in_sem.at[4])
+    order_load.start()
     for i in range(4):
         load(i).start()
+    order_load.wait()
     order = order_ref[...] - lax.axis_index("seq") * ROWS
     place = onehot(iota((ROWS, ROWS), 0) == order)
     for i in range(4):
@@ -606,6 +654,7 @@
 def on_device(n, query_points, key_points, value_points, cotangent, hilbert_order):
     shape = jax.ShapeDtypeStruct((ROWS, FEAT), BF16)
     scratch = [
+        ((1, ROWS), jnp.int32),
         ((4, ROWS, FEAT), BF16),
         ((4, ROWS, FEAT), BF16),
         ((BLK, ROWS), BF16),
@@ -647,7 +696,7 @@
     held = pl.pallas_call(
         functools.partial(kernel, n),
         out_shape=jax.ShapeDtypeStruct((4, ROWS, FEAT), BF16),
-        in_specs=[pl.BlockSpec(memory_space=pltpu.VMEM)] + [pl.BlockSpec(memory_space=pltpu.HBM)] * 4,
+        in_specs=[pl.BlockSpec(memory_space=pltpu.HBM)] * 5,
         out_specs=anywhere,
         scratch_shapes=[pltpu.VMEM(dims, kind) for dims, kind in scratch]
         + [
@@ -655,7 +704,7 @@
             pltpu.SemaphoreType.DMA((2, 5)),
             pltpu.SemaphoreType.DMA((3, 10)),
             pltpu.SemaphoreType.DMA((3, SLOTS)),
-            pltpu.SemaphoreType.DMA((4,)),
+            pltpu.SemaphoreType.DMA((5,)),
             pltpu.SemaphoreType.DMA((4,)),
         ],
         compiler_params=pltpu.CompilerParams(
@@ -664,18 +713,25 @@
         cost_estimate=pl.CostEstimate(
             flops=8_000_000_000, bytes_accessed=4 * 1024 * 1024, transcendentals=2_500_000
         ),
-    )(order, *[pltpu.with_memory_space_constraint(x, pltpu.HBM) for x in (query_points, key_points, value_points, cotangent)])
+    )(
+        *[
+            pltpu.with_memory_space_constraint(x, pltpu.HBM)
+            for x in (order, query_points, key_points, value_points, cotangent)
+        ]
+    )
     return pl.pallas_call(
         placing,
         out_shape=(shape,) * 4,
-        in_specs=[pl.BlockSpec(memory_space=pltpu.VMEM), anywhere],
+        in_specs=[pl.BlockSpec(memory_space=pltpu.HBM), anywhere],
         out_specs=(anywhere,) * 4,
-        scratch_shapes=[pltpu.VMEM((4, ROWS, FEAT), BF16)] * 2 + [pltpu.SemaphoreType.DMA((4,))] * 2,
+        scratch_shapes=[pltpu.VMEM((1, ROWS), jnp.int32)]
+        + [pltpu.VMEM((4, ROWS, FEAT), BF16)] * 2
+        + [pltpu.SemaphoreType.DMA((5,)), pltpu.SemaphoreType.DMA((4,))],
         compiler_params=pltpu.CompilerParams(vmem_limit_bytes=16 * 1024 * 1024),
         cost_estimate=pl.CostEstimate(
             flops=1_100_000_000, bytes_accessed=4 * 1024 * 1024, transcendentals=0
         ),
-    )(order, held)
+    )(pltpu.with_memory_space_constraint(order, pltpu.HBM), held)
 
 
 def solution(mesh):

time: 49.8 us -> 45.5 us (0.914)
  Pallas kernels: 48 us -> 44.6 us
  local copies, waits for them, and re-layouts: 0.67 us -> 0 us
    pallas_call x1, Pallas kernels: 45 us -> 41.1 us  [on_device(): pl.pallas_call(functools.partial(kernel, n), out_shape=jax.ShapeDtypeStru...]
    unnamed x2 -> x0, local copies, waits for them, and re-layouts: 0.67 us -> none
    pallas_call x1, Pallas kernels: 2.95 us -> 3.5 us  [on_device(): pl.pallas_call(placing, out_shape=(shape,) * 4, in_specs=[pl.BlockSpec(me...]
where the time goes in v3:
time: 45.5 us; the launch traced here: 45.4 us
  Pallas kernels  44.6 us (98%)
  between operations  0.8 us (2%)
    pallas_call x1, Pallas kernels, on_device(): pl.pallas_call(functools.partial(kernel, n), out_shape=jax.ShapeDtypeStru...  41.1 us
    pallas_call x1, Pallas kernels, on_device(): pl.pallas_call(placing, out_shape=(shape,) * 4, in_specs=[pl.BlockSpec(me...  3.5 us

profile of v3, /device:TPU:97, one launch (start us, length us, event | category | flops | bytes accessed | tf_op | source)
XLA Modules:
  0.0 45.4 jit_solution(4791040953372903542)
XLA Ops:
  0.6 41.1 %shard_map.84.held_any = bf16[4,512,512]{2,1,0:T(8,128)(2,1)S(1)} custom-call(s32[1,512]{1,0:T(1,128)} %bitcast.1, bf16[512,512]{1,0:T(8,128)(2,1)} %q_any.1, bf16[512,512]{1,0:T(8,128)(2,1)} %k_any.1, bf16[512,512]{1,0:T(8,128)(2,1)} %v_any.1, bf16[512,512]{1,0:T(8,128)(2,1)} %dz_any.1), custom_call_target="tpu_custom_call" | custom-call | flops 8000000000 | bytes 4194304 | tf_op jit(solution)/shard_map/pallas_call | solution.py:696
  41.7 3.5 %shard_map.85 = (bf16[512,512]{1,0:T(8,128)(2,1)}, bf16[512,512]{1,0:T(8,128)(2,1)}, bf16[512,512]{1,0:T(8,128)(2,1)}, bf16[512,512]{1,0:T(8,128)(2,1)}) custom-call(s32[1,512]{1,0:T(1,128)} %bitcast.2, bf16[4,512,512]{2,1,0:T(8,128)(2,1)S(1)} %shard_map.84.held_any), custom_call_target="tpu_custom_call" | custom-call | flops 1100000000 | bytes 4194304 | tf_op jit(solution)/shard_map/pallas_call | solution.py:722

commit v4 on v3

--- a/solution.py
+++ b/solution.py
@@ -126,15 +126,17 @@
     right = lax.rem(me + 1, n)
     core = lax.rem(me, 2)
     half = lax.rem(me // 2, 2)
+    odd = lax.rem(me // 4, 2)
     base = 4 * (me // 4 - 1)
     sibling = me + 1 - 2 * core
     chips = [0, 1, 3 - half, 4, 5]
-    peers = [lax.rem(base + 2 * chip + core + n, n) for chip in chips]
-    far_dense = [half + 3, half + 3, 2, half, half]
-
-    has_prev = me >= 4
-    has_next = me < n - 4
-    reach = [has_prev, has_prev, me >= 0, has_next, has_next]
+    inline = [2, 3 - 3 * odd, 4 - 3 * odd]
+    across = [3 * odd, 1 + 3 * odd]
+    peers = [base + 2 * chip + core for chip in (3 - half, 4 - 4 * odd, 5 - 4 * odd)]
+    row_to = me + 8 - 16 * odd
+    row_from = me - 8 + 16 * odd
+    to_row = (row_to >= 0) & (row_to < n)
+    from_row = (row_from >= 0) & (row_from < n)
     near = [me > 0, me < n - 1]
 
     barrier = pltpu.get_barrier_semaphore()
@@ -142,9 +144,11 @@
     def greet(device):
         pl.semaphore_signal(barrier, inc=1, device_id=(device,), device_id_type=MESH)
 
-    for device, there in zip([left, right] + peers, near + reach):
+    for device in peers:
+        greet(device)
+    for device, there in ((left, near[0]), (right, near[1]), (row_to, to_row), (row_from, from_row)):
         pl.when(there)(functools.partial(greet, device))
-    partners = sum(there.astype(jnp.int32) for there in near + reach)
+    partners = 3 + sum(there.astype(jnp.int32) for there in near + [to_row, from_row])
 
     def load(i):
         return pltpu.make_async_copy((k_any, v_any, q_any, dz_any)[i], inputs.at[i], in_sem.at[i])
@@ -175,9 +179,9 @@
         )
 
     def kv1_copy(side):
-        dst, to = [(768, right), (1024, left)][side]
+        src, dst, to = [(OWN1, 768, right), (OWN1 + 32, 1056, left)][side]
         return remote(
-            kv.at[:, pl.ds(OWN1, BLK)], kv.at[:, pl.ds(dst, BLK)],
+            kv.at[:, pl.ds(src, 96)], kv.at[:, pl.ds(dst, 96)],
             nb_send.at[side, 1], nb_recv.at[side, 1], to,
         )
 
@@ -205,19 +209,25 @@
             return q2own, q2win.at[slot_rows(slot)]
         return g2own, g2win.at[slot_rows(slot)]
 
-    def direct_copy(phase, j):
-        slot = 2 * far_dense[j] + core
+    def direct_copy(phase, i):
+        slot = 2 * (2 if i == 0 else half + 3 * odd) + core
         src, dst = far_refs(phase, slot)
-        return remote(src, dst, l2_send.at[phase, j], l2_recv.at[phase, slot], peers[j])
+        return remote(src, dst, l2_send.at[phase, i], l2_recv.at[phase, slot], peers[i])
+
+    def row_copy(phase, i):
+        slot = 2 * across[i] + core
+        _, src = far_refs(phase, 2 * inline[1 + i] + core)
+        _, dst = far_refs(phase, slot)
+        return remote(src, dst, l2_send.at[phase, 3 + i], l2_recv.at[phase, slot], row_to)
 
     def arrival(phase, slot):
         src, dst = far_refs(phase, slot)
         return remote(src, dst, l2_send.at[phase, 0], l2_recv.at[phase, slot], sibling)
 
-    def relay_copy(phase, j):
-        slot = 2 * j + core
+    def relay_copy(phase, i):
+        slot = 2 * (inline + across)[i] + core
         _, dst = far_refs(phase, slot)
-        return remote(dst, dst, l2_send.at[phase, 5 + j], l2_recv.at[phase, slot], sibling)
+        return remote(dst, dst, l2_send.at[phase, 5 + i], l2_recv.at[phase, slot], sibling)
 
     def send(copies):
         for side in range(2):
@@ -232,20 +242,37 @@
             pl.when(near[1 - side])(copies(side).wait_send)
 
     def far_send(phase):
-        for j in range(5):
-            pl.when(reach[j])(direct_copy(phase, j).start)
+        for i in range(3):
+            direct_copy(phase, i).start()
 
     def far_relay(phase):
-        for j in range(5):
-            def step(j=j):
-                arrival(phase, 2 * j + core).wait_recv()
-                relay_copy(phase, j).start()
-
-            pl.when(reach[j])(step)
+        for i in (1, 2, 0):
+            arrival(phase, 2 * inline[i] + core).wait_recv()
+            if i:
+                pl.when(to_row)(row_copy(phase, i - 1).start)
+            relay_copy(phase, i).start()
+
+    def far_relay_across(phase):
+        for i in range(2):
+            def step(i=i):
+                arrival(phase, 2 * across[i] + core).wait_recv()
+                relay_copy(phase, 3 + i).start()
+
+            pl.when(from_row)(step)
 
     def far_receive(phase):
-        for j in range(5):
-            pl.when(reach[j])(arrival(phase, 2 * j + 1 - core).wait_recv)
+        for i in range(3):
+            arrival(phase, 2 * inline[i] + 1 - core).wait_recv()
+        for i in range(2):
+            pl.when(from_row)(arrival(phase, 2 * across[i] + 1 - core).wait_recv)
+
+    def far_sent(phase):
+        for i in range(3):
+            direct_copy(phase, i).wait_send()
+            relay_copy(phase, i).wait_send()
+        for i in range(2):
+            pl.when(to_row)(row_copy(phase, i).wait_send)
+            pl.when(from_row)(relay_copy(phase, 3 + i).wait_send)
 
     def clear(rows):
         for first in rows:
@@ -260,14 +287,6 @@
         kv2[:, first : first + 128] = jnp.zeros((2, 128, FEAT), BF16)
         q2win[first : first + 128] = jnp.zeros((128, FEAT), BF16)
         g2win[first : first + 128] = jnp.zeros((128, 640), BF16)
-
-    for side in range(2):
-        pl.when(jnp.logical_not(near[side]))(functools.partial(clear_side, side))
-    pl.when(jnp.logical_not(has_prev))(functools.partial(clear_far, 0))
-    pl.when(jnp.logical_not(has_next))(functools.partial(clear_far, 192))
-    kv2[:, 320:384] = jnp.zeros((2, 64, FEAT), BF16)
-    q2win[320:384] = jnp.zeros((64, FEAT), BF16)
-    g2win[320:384] = jnp.zeros((64, 640), BF16)
 
     order_load.wait()
     order = order_ref[...] - me * ROWS
@@ -276,22 +295,32 @@
     gather = jnp.concatenate(
         [jnp.where(column == lane + float(BLK * i), 1.0, 0.0).astype(BF16) for i in range(4)], axis=1
     )
-    pool1[...] = onehot(iota((BLK, ROWS), 0) == (iota((BLK, ROWS), 1) >> 2))
-    pool1t[...] = onehot((iota((ROWS, BLK), 0) >> 2) == iota((ROWS, BLK), 1))
+
     pool2[...] = onehot((iota((256, ROWS), 0) & 31) == (iota((256, ROWS), 1) >> 4))
-    pool2t[...] = onehot((iota((ROWS, 256), 0) >> 4) == (iota((ROWS, 256), 1) & 31))
 
     for which in range(2):
         load(which).wait()
         kv[which, 128:640] = nn(gather, inputs[which]).astype(BF16)
+    kv2own[0] = (nn(pool2[0:32], kv[0, 128:640]) * (1.0 / 16)).astype(BF16)
+    kv2own[1] = nn(pool2[0:32], kv[1, 128:640]).astype(BF16)
     pl.semaphore_wait(barrier, partners)
+    far_send(0)
     send(kv0_copy)
+    pool1[...] = onehot(iota((BLK, ROWS), 0) == (iota((BLK, ROWS), 1) >> 2))
     kv[0, OWN1 : OWN1 + BLK] = (nn(pool1[...], kv[0, 128:640]) * 0.25).astype(BF16)
     kv[1, OWN1 : OWN1 + BLK] = nn(pool1[...], kv[1, 128:640]).astype(BF16)
     send(kv1_copy)
-    kv2own[0] = (nn(pool2[0:32], kv[0, 128:640]) * (1.0 / 16)).astype(BF16)
-    kv2own[1] = nn(pool2[0:32], kv[1, 128:640]).astype(BF16)
-    far_send(0)
+    pool1t[...] = onehot((iota((ROWS, BLK), 0) >> 2) == iota((ROWS, BLK), 1))
+    pool2t[...] = onehot((iota((ROWS, 256), 0) >> 4) == (iota((ROWS, 256), 1) & 31))
+
+    for side in range(2):
+        pl.when(jnp.logical_not(near[side]))(functools.partial(clear_side, side))
+    pl.when(me < 4)(functools.partial(clear_far, 0))
+    pl.when(me >= n - 4)(functools.partial(clear_far, 192))
+    kv2[:, 320:384] = jnp.zeros((2, 64, FEAT), BF16)
+    q2win[320:384] = jnp.zeros((64, FEAT), BF16)
+    g2win[320:384] = jnp.zeros((64, 640), BF16)
+
     load(2).wait()
     query = (nn(gather, inputs[2]) * SCALE).astype(BF16)
     q2own[...] = (nn(pool2[0:32], query) * (1.0 / 16)).astype(BF16)
@@ -377,11 +406,17 @@
 
     forward_inner(range(4))
 
+    far_relay(0)
     receive(kv0_copy)
+    for which in range(2):
+        scale = 0.25 if which == 0 else 1.0
+        for source, target in ((0, 864), (640, 1024)):
+            pooled = nn(pool1[0:32, 0:BLK], kv[which, source : source + BLK])
+            kv[which, target : target + 32] = (pooled * scale).astype(BF16)
     receive(kv1_copy)
     send(lambda side: qg_copy(side, 0))
-    far_relay(0)
     far_send(1)
+    far_relay_across(0)
     for which in range(2):
         kvt[which, :, 0:128] = jnp.transpose(kv[which, 0:128])
         kvt[which, :, 640:1152] = jnp.transpose(kv[which, 640:1152])
@@ -475,9 +510,10 @@
         term = nn(chosen, target)
         packed = term if packed is None else packed + term
     g2own[:, FEAT:] = packed.astype(BF16)
+    far_send(2)
     send(stats_copy)
     send(lambda side: qg_copy(side, 1))
-    far_send(2)
+    far_relay(1)
 
     def pair_row(ref, pair):
         return jnp.concatenate([ref[pl.ds(2 * pair + e, 1), :] for e in range(2)], axis=1)
@@ -520,9 +556,8 @@
             grads_of(sums_of[i // 5], *unit, diff)
 
     backward(range(4))
-
-    far_relay(1)
     far_relay(2)
+    far_relay_across(1)
 
     mixing2 = nn(kv2[1], g2m[...])
     diff2 = (weights2[...] * (mixing2 - energy2)).astype(BF16)
@@ -588,6 +623,14 @@
 
     from_halo(range(4))
 
+    far_relay_across(2)
+
+    def spread_rows(matrix, x):
+        high, low = parts_of(x, 2)
+        return nn(matrix, high) + nn(matrix, low)
+
+    dkv[0, 0:ROWS] += spread_rows(pool1t[...], dkv[0, ROWS:] * 0.25)
+    dkv[1, 0:ROWS] += spread_rows(pool1t[...], dkv[1, ROWS:])
     far_receive(1)
     far_receive(2)
     far_stats = g2win[:, FEAT:]
@@ -603,25 +646,17 @@
     dk2 = jnp.where(lane_head, nn(jnp.transpose(far_diff), q2win[...]), 0.0)
     dv2 = jnp.where(lane_head, nn(jnp.transpose(far_weight.astype(BF16)), g2win[:, 0:FEAT]), 0.0)
 
-    def spread_rows(matrix, x):
-        high, low = parts_of(x, 2)
-        return nn(matrix, high) + nn(matrix, low)
-
-    key_grad = dkv[0, 0:ROWS] + spread_rows(pool1t[...], dkv[0, ROWS:] * 0.25)
-    key_grad = key_grad + spread_rows(pool2t[...], dk2 * (1.0 / 16))
+    key_grad = dkv[0, 0:ROWS] + spread_rows(pool2t[...], dk2 * (1.0 / 16))
     outputs[2] = key_grad.astype(BF16)
     store(2).start()
-    value_grad = dkv[1, 0:ROWS] + spread_rows(pool1t[...], dkv[1, ROWS:])
-    value_grad = value_grad + spread_rows(pool2t[...], dv2)
+    value_grad = dkv[1, 0:ROWS] + spread_rows(pool2t[...], dv2)
     outputs[3] = value_grad.astype(BF16)
     store(3).start()
 
     for copies in (kv0_copy, kv1_copy, lambda side: qg_copy(side, 0), lambda side: qg_copy(side, 1), stats_copy):
         sent(copies)
     for phase in range(3):
-        for j in range(5):
-            pl.when(reach[j])(direct_copy(phase, j).wait_send)
-            pl.when(reach[j])(relay_copy(phase, j).wait_send)
+        far_sent(phase)
     for i in range(4):
         store(i).wait()
 

time: 45.5 us -> 40.8 us (0.90)
  Pallas kernels: 44.6 us -> 39.9 us
    pallas_call x1, Pallas kernels: 41.1 us -> 36.4 us  [on_device(): pl.pallas_call(functools.partial(kernel, n), out_shape=jax.ShapeDtypeStru...]
where the time goes in v4:
time: 40.8 us; the launch traced here: 40.7 us
  Pallas kernels  39.9 us (98%)
  between operations  0.8 us (2%)
    pallas_call x1, Pallas kernels, on_device(): pl.pallas_call(functools.partial(kernel, n), out_shape=jax.ShapeDtypeStru...  36.4 us
    pallas_call x1, Pallas kernels, on_device(): pl.pallas_call(placing, out_shape=(shape,) * 4, in_specs=[pl.BlockSpec(me...  3.5 us

profile of v4, /device:TPU:97, one launch (start us, length us, event | category | flops | bytes accessed | tf_op | source)
XLA Modules:
  0.0 40.7 jit_solution(5765026926026404082)
XLA Ops:
  0.6 36.4 %shard_map.84.held_any = bf16[4,512,512]{2,1,0:T(8,128)(2,1)S(1)} custom-call(s32[1,512]{1,0:T(1,128)} %bitcast.1, bf16[512,512]{1,0:T(8,128)(2,1)} %q_any.1, bf16[512,512]{1,0:T(8,128)(2,1)} %k_any.1, bf16[512,512]{1,0:T(8,128)(2,1)} %v_any.1, bf16[512,512]{1,0:T(8,128)(2,1)} %dz_any.1), custom_call_target="tpu_custom_call" | custom-call | flops 8000000000 | bytes 4194304 | tf_op jit(solution)/shard_map/pallas_call | solution.py:731
  37.0 3.5 %shard_map.85 = (bf16[512,512]{1,0:T(8,128)(2,1)}, bf16[512,512]{1,0:T(8,128)(2,1)}, bf16[512,512]{1,0:T(8,128)(2,1)}, bf16[512,512]{1,0:T(8,128)(2,1)}) custom-call(s32[1,512]{1,0:T(1,128)} %bitcast.2, bf16[4,512,512]{2,1,0:T(8,128)(2,1)S(1)} %shard_map.84.held_any), custom_call_target="tpu_custom_call" | custom-call | flops 1100000000 | bytes 4194304 | tf_op jit(solution)/shard_map/pallas_call | solution.py:757

commit v5 on v4

--- a/solution.py
+++ b/solution.py
@@ -661,24 +661,18 @@
         store(i).wait()
 
 
-def placing(order_any, held_any, out_ref, dq_ref, dk_ref, dv_ref, order_ref, held, results, in_sem, out_sem):
+def placing(order_any, held, out_ref, dq_ref, dk_ref, dv_ref, order_ref, results, in_sem, out_sem):
     targets = (out_ref, dq_ref, dk_ref, dv_ref)
-
-    def load(i):
-        return pltpu.make_async_copy(held_any.at[i], held.at[i], in_sem.at[i])
 
     def store(i):
         return pltpu.make_async_copy(results.at[i], targets[i], out_sem.at[i])
 
-    order_load = pltpu.make_async_copy(order_any, order_ref, in_sem.at[4])
+    order_load = pltpu.make_async_copy(order_any, order_ref, in_sem.at[0])
     order_load.start()
-    for i in range(4):
-        load(i).start()
     order_load.wait()
     order = order_ref[...] - lax.axis_index("seq") * ROWS
     place = onehot(iota((ROWS, ROWS), 0) == order)
     for i in range(4):
-        load(i).wait()
         product = nt if i < 2 else nn
         results[i] = product(place, held[i]).astype(BF16)
         store(i).start()
@@ -757,11 +751,11 @@
     return pl.pallas_call(
         placing,
         out_shape=(shape,) * 4,
-        in_specs=[pl.BlockSpec(memory_space=pltpu.HBM), anywhere],
+        in_specs=[pl.BlockSpec(memory_space=pltpu.HBM), pl.BlockSpec(memory_space=pltpu.VMEM)],
         out_specs=(anywhere,) * 4,
         scratch_shapes=[pltpu.VMEM((1, ROWS), jnp.int32)]
-        + [pltpu.VMEM((4, ROWS, FEAT), BF16)] * 2
-        + [pltpu.SemaphoreType.DMA((5,)), pltpu.SemaphoreType.DMA((4,))],
+        + [pltpu.VMEM((4, ROWS, FEAT), BF16)]
+        + [pltpu.SemaphoreType.DMA((1,)), pltpu.SemaphoreType.DMA((4,))],
         compiler_params=pltpu.CompilerParams(vmem_limit_bytes=16 * 1024 * 1024),
         cost_estimate=pl.CostEstimate(
             flops=1_100_000_000, bytes_accessed=4 * 1024 * 1024, transcendentals=0

time: 40.8 us -> 40.1 us (0.983)
  Pallas kernels: 39.9 us -> 39.2 us
    pallas_call x1, Pallas kernels: 3.5 us -> 2.81 us  [on_device(): pl.pallas_call(placing, out_shape=(shape,) * 4, in_specs=[pl.BlockSpec(me...]
where the time goes in v5:
time: 40.1 us; the launch traced here: 40 us
  Pallas kernels  39.2 us (98%)
  between operations  0.8 us (2%)
    pallas_call x1, Pallas kernels, on_device(): pl.pallas_call(functools.partial(kernel, n), out_shape=jax.ShapeDtypeStru...  36.4 us
    pallas_call x1, Pallas kernels, on_device(): pl.pallas_call(placing, out_shape=(shape,) * 4, in_specs=[pl.BlockSpec(me...  2.81 us

profile of v5, /device:TPU:97, one launch (start us, length us, event | category | flops | bytes accessed | tf_op | source)
XLA Modules:
  0.0 40.0 jit_solution(12253402792264674141)
XLA Ops:
  0.6 36.4 %shard_map.84.held = bf16[4,512,512]{2,1,0:T(8,128)(2,1)S(1)} custom-call(s32[1,512]{1,0:T(1,128)} %bitcast.1, bf16[512,512]{1,0:T(8,128)(2,1)} %q_any.1, bf16[512,512]{1,0:T(8,128)(2,1)} %k_any.1, bf16[512,512]{1,0:T(8,128)(2,1)} %v_any.1, bf16[512,512]{1,0:T(8,128)(2,1)} %dz_any.1), custom_call_target="tpu_custom_call" | custom-call | flops 8000000000 | bytes 4194304 | tf_op jit(solution)/shard_map/pallas_call | solution.py:725
  37.0 2.8 %shard_map.85 = (bf16[512,512]{1,0:T(8,128)(2,1)}, bf16[512,512]{1,0:T(8,128)(2,1)}, bf16[512,512]{1,0:T(8,128)(2,1)}, bf16[512,512]{1,0:T(8,128)(2,1)}) custom-call(s32[1,512]{1,0:T(1,128)} %bitcast.2, bf16[4,512,512]{2,1,0:T(8,128)(2,1)S(1)} %shard_map.84.held), custom_call_target="tpu_custom_call" | custom-call | flops 1100000000 | bytes 4194304 | tf_op jit(solution)/shard_map/pallas_call | solution.py:751
